TPU v7x, 256 devices: a whole 4x4x8 slice. The times are simulated.
256 devices in a mesh: gx: 16 (over z, core), gy: 16 (over y, x).
Axes of the slice: x: 4, y: 4, z: 8, core: 2. Of those that a mesh axis runs over, the one named last changes fastest.
Arguments:
- populations: float32 [19, 256, 128, 256], P(None, 'gx', 'gy'), may hold values from 0 to 0.5, as said below
- relax_rate: float32 [256, 128, 256], P('gx', 'gy'), may hold values from 0.6 to 1.6
- solid_mask: int32 [256, 128, 256], P('gx', 'gy'), may hold values 0 or 1
- singular_values: float32 [64], replicated, may hold values from 1 to 4
- basis: float32 [64, 3, 128, 64, 128], P(None, None, 'gx', 'gy'), may hold values from -60 to 60
- snapshots: float32 [15, 3, 128, 64, 128], P(None, None, 'gx', 'gy'), may hold values from -60 to 60
Outputs:
- populations_out: float32 [19, 256, 128, 256], P(None, 'gx', 'gy')
- upper_factor: float32 [80, 80], replicated
- new_basis: float32 [80, 3, 128, 64, 128], P(None, None, 'gx', 'gy')
Inputs may be any that keep to these rules, and one draw needn't show every extreme that they name: `populations`: each entry is w_i times a factor between 0.7 and 1.3.
All inputs are finite; a program needn't handle non-finite values. No bound on the sum of `solid_mask` on one device may be relied on, other than what follows from the above.
Results may differ from a plain program's by a relative error of at most 0.00012.
Values sent between devices are 32-bit elements; how exact they have to be, the bound alone decides.
A program may use at most 128 MiB of HBM per device.

v0:
```python
import functools

import jax
import jax.numpy as jnp
from jax import lax
from jax.experimental import pallas as pl
from jax.experimental.pallas import tpu as pltpu
from jax.sharding import PartitionSpec as P

MESH = pl.DeviceIdType.MESH
HIGHEST = lax.Precision.HIGHEST
F32 = jnp.float32
BF16 = jnp.bfloat16

VELOCITY = [
    (0, 0, 0),
    (1, 0, 0),
    (-1, 0, 0),
    (0, 1, 0),
    (0, -1, 0),
    (0, 0, 1),
    (0, 0, -1),
    (1, 1, 0),
    (-1, -1, 0),
    (1, -1, 0),
    (-1, 1, 0),
    (1, 0, 1),
    (-1, 0, -1),
    (1, 0, -1),
    (-1, 0, 1),
    (0, 1, 1),
    (0, -1, -1),
    (0, 1, -1),
    (0, -1, 1),
]
SPEED_SCALE = 10.0

ORDER = [1, 7, 9, 11, 13, 2, 8, 10, 12, 14, 0, 3, 4, 5, 6, 15, 16, 17, 18]
PLACE = [ORDER.index(i) for i in range(19)]
Y_UP = [3, 7, 10, 15, 17]
Y_DOWN = [4, 8, 9, 16, 18]
CORNERS = [(7, 16, 1, 1), (8, 1, -1, -1), (9, 16, 1, -1), (10, 1, -1, 1)]

NX, NY, NZ = 16, 8, 256
XC, YC, ZC = 8, 4, 128
COLS, RANK, OLD = 80, 64, 15
ROWS = 3 * XC * YC
HALO0 = 8


def flow(field):
    plus = [field[i] + field[i + 1] for i in range(1, 19, 2)]
    diff = [field[i] - field[i + 1] for i in range(1, 19, 2)]
    rho = field[0]
    for s in plus:
        rho = rho + s
    comps = []
    for axis in range(3):
        total = None
        for p, d in enumerate(diff):
            c = VELOCITY[2 * p + 1][axis]
            if c:
                total = d if total is None else (total + d if c > 0 else total - d)
        comps.append(total)
    inv = 1.0 / rho
    return rho, [c * inv for c in comps]


def collide(field, rate, solid):
    rho, vel = flow(field)
    tri = [3.0 * u for u in vel]
    base = 1.0 - 1.5 * (vel[0] * vel[0] + vel[1] * vel[1] + vel[2] * vel[2])
    post = [None] * 19
    face = rho * (1.0 / 18.0)
    edge = rho * (1.0 / 36.0)
    rest = rho * (1.0 / 3.0) * base
    post[0] = jnp.where(solid, field[0], field[0] + rate * (rest - field[0]))
    for i in range(1, 19, 2):
        along = None
        for axis in range(3):
            c = VELOCITY[i][axis]
            if c:
                along = (
                    tri[axis]
                    if along is None
                    else (along + tri[axis] if c > 0 else along - tri[axis])
                )
        weight = face if i < 7 else edge
        even = weight * (base + 0.5 * (along * along))
        odd = weight * along
        fp, fm = field[i], field[i + 1]
        post[i] = jnp.where(solid, fm, fp + rate * ((even + odd) - fp))
        post[i + 1] = jnp.where(solid, fp, fm + rate * ((even - odd) - fm))
    return post


def arrive(post_ref, up_ref, down_ref, x):
    row = lax.broadcasted_iota(jnp.int32, (NY, NZ), 0)
    field = []
    for i, (cx, cy, cz) in enumerate(VELOCITY):
        v = post_ref[PLACE[i], x + 1 - cx]
        if cy == 1:
            halo = up_ref[Y_UP.index(i), pl.ds(x + HALO0 - cx, 1), :]
            v = jnp.where(row == 0, halo, pltpu.roll(v, 1, axis=0))
        elif cy == -1:
            halo = down_ref[Y_DOWN.index(i), pl.ds(x + HALO0 - cx, 1), :]
            v = jnp.where(row == NY - 1, halo, pltpu.roll(v, NY - 1, axis=0))
        if cz == 1:
            v = pltpu.roll(v, 1, axis=1)
        elif cz == -1:
            v = pltpu.roll(v, NZ - 1, axis=1)
        field.append(v)
    return field


def split(x):
    hi = x.astype(BF16)
    lo = (x - hi.astype(F32)).astype(BF16)
    return hi, lo


def dot(a, b, ca, cb, precision=None):
    return lax.dot_general(
        a, b, (((ca,), (cb,)), ((), ())), precision=precision, preferred_element_type=F32
    )


def scale_row(ref, sv_ref):
    ref[...] = jnp.ones_like(ref)
    ref[0:1, 0:RANK] = sv_ref[...]
    return ref[0:1, :]


def main_kernel(
    nx,
    ny,
    pops_hbm,
    rate_hbm,
    mask_hbm,
    sv_ref,
    basis_hbm,
    snaps_hbm,
    field_hbm,
    coarse_ref,
    inverse_ref,
    upper_ref,
    border_ref,
    pops,
    rate,
    mask,
    stack,
    post_a,
    post_b,
    out_up,
    out_down,
    in_up,
    in_down,
    in_corner,
    vel,
    pooled,
    gram,
    parts,
    recv_a,
    send_b,
    recv_b,
    recv_c,
    vec_a,
    vec_b,
    vec_in_a,
    vec_in_b,
    scale,
    plane_sem,
    load_sem,
    store_sem,
    halo_send,
    halo_recv,
    red_send,
    red_recv,
):
    mx, my = lax.axis_index("gx"), lax.axis_index("gy")
    owners = COLS // 8
    posts = (post_a, post_b)

    def shifted(dx, dy):
        return (lax.rem(mx + (dx + nx), nx), lax.rem(my + (dy + ny), ny))

    def load_plane(x):
        return pltpu.make_async_copy(pops_hbm.at[:, x], pops.at[:, x], plane_sem.at[x])

    loads = [
        pltpu.make_async_copy(rate_hbm, rate, load_sem.at[0]),
        pltpu.make_async_copy(mask_hbm, mask, load_sem.at[1]),
        pltpu.make_async_copy(basis_hbm, stack.at[pl.ds(0, RANK)], load_sem.at[2]),
        pltpu.make_async_copy(snaps_hbm, stack.at[pl.ds(RANK, OLD)], load_sem.at[3]),
    ]
    loads[0].start()
    loads[1].start()

    @pl.loop(0, NX)
    def _(x):
        load_plane(x).start()

    loads[2].start()
    loads[3].start()

    barrier = pltpu.get_barrier_semaphore()

    @pl.loop(1, nx)
    def _(j):
        pl.semaphore_signal(
            barrier, inc=1, device_id=(lax.rem(mx + j, nx), my), device_id_type=MESH
        )

    @pl.loop(1, ny)
    def _(j):
        pl.semaphore_signal(
            barrier, inc=1, device_id=(mx, lax.rem(my + j, ny)), device_id_type=MESH
        )

    for dx in (-1, 1):
        for dy in (-1, 1):
            pl.semaphore_signal(barrier, inc=1, device_id=shifted(dx, dy), device_id_type=MESH)

    stack[COLS - 1] = jnp.zeros((ROWS, ZC), F32)

    def put(post, step, x):
        for i in range(19):
            posts[step][PLACE[i], x + 1] = post[i]
        for p, i in enumerate(Y_UP):
            out_up[step, p, pl.ds(x, 1), :] = post[i][NY - 1 : NY, :]
        for p, i in enumerate(Y_DOWN):
            out_down[step, p, pl.ds(x, 1), :] = post[i][0:1, :]

    def halo(step):
        post = posts[step]
        inner = pl.ds(HALO0, NX)
        moves = [
            (post.at[pl.ds(0, 5), NX], post.at[pl.ds(0, 5), 0], (1, 0)),
            (post.at[pl.ds(5, 5), 1], post.at[pl.ds(5, 5), NX + 1], (-1, 0)),
            (out_up.at[step], in_up.at[step, :, inner, :], (0, 1)),
            (out_down.at[step], in_down.at[step, :, inner, :], (0, -1)),
        ]
        for c, (i, plane, dx, dy) in enumerate(CORNERS):
            moves.append((post.at[PLACE[i], plane], in_corner.at[step, c], (dx, dy)))
        return [
            pltpu.make_async_remote_copy(
                src_ref=src,
                dst_ref=dst,
                send_sem=halo_send.at[step, k],
                recv_sem=halo_recv.at[step, k],
                device_id=shifted(*to),
                device_id_type=MESH,
            )
            for k, (src, dst, to) in enumerate(moves)
        ]

    def land(step):
        for c, (i, plane, dx, dy) in enumerate(CORNERS):
            at = HALO0 - 1 if dx == 1 else HALO0 + NX
            if dy == 1:
                in_up[step, Y_UP.index(i), at : at + 1, :] = in_corner[step, c, NY - 1 : NY, :]
            else:
                in_down[step, Y_DOWN.index(i), at : at + 1, :] = in_corner[step, c, 0:1, :]

    loads[0].wait()
    loads[1].wait()

    @pl.loop(0, NX)
    def _(x):
        load_plane(x).wait()
        field = [pops[i, x] for i in range(19)]
        put(collide(field, rate[x], mask[x] > 0), 0, x)

    pl.semaphore_wait(barrier, (nx - 1) + (ny - 1) + 4)
    first = halo(0)
    for copy in first:
        copy.start()

    loads[2].wait()
    loads[3].wait()
    rows = stack.reshape(COLS * ROWS, ZC)
    gram[...] = jnp.zeros_like(gram)
    wide = 8

    @pl.loop(0, ROWS // wide)
    def _(c):
        tall = jnp.concatenate(
            [rows[pl.ds(c * wide + w, COLS, stride=ROWS), :] for w in range(wide)], axis=1
        )
        hi, lo = split(tall)
        gram[:, 0:COLS] += dot(jnp.concatenate([hi, lo], axis=0), hi, 1, 1)

    parts[0:COLS, :] = gram[0:COLS, :]
    low = jnp.concatenate([gram[COLS : 2 * COLS, :], jnp.zeros((ZC - COLS, ZC), F32)], axis=0)
    parts[...] = gram[0:COLS, :] + low[0:COLS] + jnp.transpose(low)[0:COLS]

    def to_owner(j):
        peer = lax.rem(mx + j, nx)
        chunk = lax.rem(peer, owners)
        return peer, pltpu.make_async_remote_copy(
            src_ref=parts.at[pl.ds(pl.multiple_of(chunk * 8, 8), 8)],
            dst_ref=recv_a.at[mx],
            send_sem=red_send.at[0],
            recv_sem=red_recv.at[0],
            device_id=(peer, my),
            device_id_type=MESH,
        )

    @pl.loop(1, nx)
    def _(j):
        peer, copy = to_owner(j)

        @pl.when(peer < owners)
        def _():
            copy.start()

    own = pl.ds(pl.multiple_of(lax.rem(mx, owners) * 8, 8), 8)
    recv_a[mx] = parts[own, :]

    for copy in first:
        copy.wait_recv()
    land(0)

    @pl.loop(0, NX)
    def _(x):
        field = arrive(post_a, in_up.at[0], in_down.at[0], x)
        put(collide(field, rate[x], mask[x] > 0), 1, x)

    second = halo(1)
    for copy in second:
        copy.start()

    def all_along(src, dst, k, axis):
        def copy(j):
            if axis == 0:
                peer = (lax.rem(mx + j, nx), my)
            else:
                peer = (mx, lax.rem(my + j, ny))
            return pltpu.make_async_remote_copy(
                src_ref=src,
                dst_ref=dst,
                send_sem=red_send.at[k],
                recv_sem=red_recv.at[k],
                device_id=peer,
                device_id_type=MESH,
            )

        return copy

    def start_all(copy, count):
        @pl.loop(1, count)
        def _(j):
            copy(j).start()

    def wait_for(ref, sem):
        pltpu.make_async_copy(ref, ref, sem).wait()

    def total(ref, count):
        value = ref[0]
        for j in range(1, count):
            value = value + ref[j]
        return value

    ring_b = all_along(send_b.at[0], recv_b.at[my], 1, 1)
    ring_c = all_along(send_b.at[1], recv_c.at[mx], 2, 0)

    @pl.when(mx < owners)
    def _():
        wait_for(recv_a.at[pl.ds(0, nx - 1)], red_recv.at[0])
        value = total(recv_a, nx)
        send_b[0] = value
        recv_b[my] = value
        start_all(ring_b, ny)

    for copy in second:
        copy.wait_recv()
    land(1)

    def store_plane(x):
        return pltpu.make_async_copy(pops.at[:, x], field_hbm.at[:, x], store_sem.at[x])

    @pl.loop(0, XC)
    def _(xc):
        sums = [None] * 3
        for half in range(2):
            x = 2 * xc + half
            field = arrive(post_b, in_up.at[1], in_down.at[1], x)
            for i in range(19):
                pops[i, x] = field[i]
            store_plane(x).start()
            fluid = mask[x] == 0
            for a, u in enumerate(flow(field)[1]):
                u = jnp.where(fluid, u, 0.0)
                sums[a] = u if half == 0 else sums[a] + u
        for a in range(3):
            vel[pl.ds(pl.multiple_of(a * XC * NY + xc * NY, NY), NY), :] = sums[a]

    @pl.when(mx < owners)
    def _():
        wait_for(recv_b.at[pl.ds(0, ny - 1)], red_recv.at[1])
        value = total(recv_b, ny)
        send_b[1] = value
        recv_c[mx] = value
        start_all(ring_c, nx)

    fine = lax.broadcasted_iota(jnp.int32, (NZ, ZC), 0)
    pair = lax.broadcasted_iota(jnp.int32, (NZ, ZC), 1)
    pick = jnp.where(fine // 2 == pair, SPEED_SCALE / 8.0, 0.0).astype(F32)
    pooled[...] = dot(vel[...], pick, 1, 0, HIGHEST)
    coarse = pooled[pl.ds(0, ROWS, stride=2), :] + pooled[pl.ds(1, ROWS, stride=2), :]
    coarse_ref[...] = coarse
    stack[COLS - 1] = coarse

    vec_a[...] = jnp.zeros_like(vec_a)

    @pl.loop(0, ROWS // wide)
    def _(c):
        value = vec_a[0:COLS, :]
        for w in range(wide):
            r = c * wide + w
            value = value + rows[pl.ds(r, COLS, stride=ROWS), :] * coarse_ref[pl.ds(r, 1), :]
        vec_a[0:COLS, :] = value

    last = dot(jnp.ones((8, ZC), F32), vec_a[...], 1, 1, HIGHEST)
    vec_b[0] = last
    vec_in_a[mx] = last
    ring_d = all_along(vec_b.at[0], vec_in_a.at[mx], 3, 0)
    start_all(ring_d, nx)

    @pl.when(mx < owners)
    def _():
        wait_for(recv_c.at[pl.ds(0, owners - 1)], red_recv.at[2])

    @pl.when(mx >= owners)
    def _():
        wait_for(recv_c.at[pl.ds(0, owners)], red_recv.at[2])

    row = lax.broadcasted_iota(jnp.int32, (COLS, ZC), 0)
    lane = lax.broadcasted_iota(jnp.int32, (COLS, ZC), 1)
    srow = scale_row(scale, sv_ref)
    scol = jnp.sum(jnp.where(row == lane, srow, 0.0), axis=1, keepdims=True)
    per_row = 1.0 / (all_rows(nx, ny))
    whole = jnp.concatenate([recv_c[c] for c in range(owners)], axis=0)
    whole = whole * (srow * scol) * per_row
    whole = jnp.where((row == COLS - 1) & (lane == COLS - 1), 1.0, whole)

    row8 = lax.broadcasted_iota(jnp.int32, (8, ZC), 0)
    lane8 = lax.broadcasted_iota(jnp.int32, (8, ZC), 1)

    def eight(b, state):
        a, e = state
        r, t = a[0:8], e[0:8]
        for j in range(8):
            pivot = r[j : j + 1, j : j + 1]
            inv = lax.rsqrt(pivot)
            inv = inv * (1.5 - 0.5 * pivot * inv * inv)
            factor = jnp.where(row8[:, 0:1] > j, r[:, j : j + 1] * inv, 0.0)
            urow, trow = r[j : j + 1] * inv, t[j : j + 1] * inv
            r = jnp.where(row8 == j, urow, r - factor * urow)
            t = jnp.where(row8 == j, trow, t - factor * trow)
        r = jnp.where((lane8 >= row8) & (lane8 < COLS - 8 * b), r, 0.0)
        at = pl.ds(pl.multiple_of(8 * b, 8), 8)
        upper_ref[at, :] = pltpu.roll(r, 8 * b, axis=1)
        inverse_ref[at, :] = t
        change = dot(r, jnp.concatenate([r, t], axis=1), 0, 0, HIGHEST)
        zero = jnp.zeros((8, ZC), F32)
        a = jnp.concatenate([a[8:] - change[8:COLS, 0:ZC], zero], axis=0)
        e = jnp.concatenate([e[8:] - change[8:COLS, ZC:], zero], axis=0)
        return pltpu.roll(a, ZC - 8, axis=1), e

    state = (whole, (row == lane).astype(F32))
    half = (owners + 1) // 2
    state = lax.fori_loop(0, half, eight, state)

    wait_for(vec_in_a.at[pl.ds(0, nx - 1)], red_recv.at[3])
    value = total(vec_in_a, nx)
    vec_b[1] = value
    vec_in_b[my] = value
    ring_e = all_along(vec_b.at[1], vec_in_b.at[my], 4, 1)
    start_all(ring_e, ny)

    lax.fori_loop(half, owners, eight, state)

    wait_for(vec_in_b.at[pl.ds(0, ny - 1)], red_recv.at[4])
    border_ref[...] = total(vec_in_b, ny) * srow * per_row

    @pl.loop(0, NX)
    def _(x):
        store_plane(x).wait()

    for copy in first + second:
        copy.wait_send()

    @pl.when(mx < owners)
    def _():
        wait_for(recv_a.at[pl.ds(0, owners - 1)], red_send.at[0])
        wait_for(recv_b.at[pl.ds(0, ny - 1)], red_send.at[1])
        wait_for(recv_a.at[pl.ds(0, nx - 1)], red_send.at[2])

    @pl.when(mx >= owners)
    def _():
        wait_for(recv_a.at[pl.ds(0, owners)], red_send.at[0])

    wait_for(vec_in_a.at[pl.ds(0, nx - 1)], red_send.at[3])
    wait_for(vec_in_b.at[pl.ds(0, ny - 1)], red_send.at[4])


def all_rows(nx, ny):
    return float(ROWS * ZC * nx * ny)


def finish_kernel(
    field_hbm,
    sv_ref,
    basis_hbm,
    snaps_hbm,
    coarse_ref,
    inverse_ref,
    upper_ref,
    border_ref,
    pops_hbm,
    factor_ref,
    new_hbm,
    stack,
    fresh,
    left,
    scale,
    load_sem,
    store_sem,
):
    wide = 8
    copies = [
        pltpu.make_async_copy(basis_hbm, stack.at[pl.ds(0, RANK)], load_sem.at[0]),
        pltpu.make_async_copy(snaps_hbm, stack.at[pl.ds(RANK, OLD)], load_sem.at[1]),
        pltpu.make_async_copy(field_hbm, pops_hbm, load_sem.at[2]),
    ]
    for copy in copies:
        copy.start()
    stack[COLS - 1] = coarse_ref[...]

    row = lax.broadcasted_iota(jnp.int32, (COLS, ZC), 0)
    lane = lax.broadcasted_iota(jnp.int32, (COLS, ZC), 1)
    inverse = inverse_ref[...]
    border = border_ref[...]
    lane8 = lax.broadcasted_iota(jnp.int32, (8, ZC), 1)
    old = jnp.where(lane8 < COLS - 1, border, 0.0)
    tall = jnp.concatenate([inverse, jnp.zeros((ZC - COLS, ZC), F32)], axis=0)
    lrow = dot(old, tall, 1, 1, HIGHEST)
    lrow = jnp.where(lane8 < COLS - 1, lrow, 0.0)
    wide_old = jnp.concatenate([old] * (ZC // 8), axis=0)
    lcol = dot(inverse, wide_old, 1, 1, HIGHEST)
    left_over = border[0:1, COLS - 1 : COLS] - jnp.sum(lrow[0:1] * lrow[0:1], axis=1, keepdims=True)
    inv = lax.rsqrt(left_over)
    inv = inv * (1.5 - 0.5 * left_over * inv * inv)
    diag = left_over * inv
    end = dot(lrow, tall, 1, 0, HIGHEST)[0:1]
    end = jnp.where(lane[0:1] == COLS - 1, inv, -end * inv)
    inverse = jnp.where(row == COLS - 1, end, inverse)
    final = jnp.where(lane == COLS - 1, jnp.where(row == COLS - 1, diag, lcol), upper_ref[...])
    final = jnp.where((row == COLS - 1) & (lane < COLS - 1), 0.0, final)
    factor_ref[...] = final[:, 0:COLS]

    inverse = inverse * scale_row(scale, sv_ref)
    hi = inverse.astype(BF16).astype(F32)
    lo = inverse - hi
    none = jnp.zeros_like(hi)
    hi, lo = jnp.concatenate([hi, none], axis=1), jnp.concatenate([lo, none], axis=1)
    placed = hi + pltpu.roll(lo, COLS, axis=1) + pltpu.roll(hi, 2 * COLS, axis=1)
    left[...] = placed.astype(BF16)

    rows = stack.reshape(COLS * ROWS, ZC)
    made = fresh.reshape(COLS * ROWS, ZC)

    def store(c):
        part = pl.ds(pl.multiple_of(c * wide, wide), wide)
        return pltpu.make_async_copy(fresh.at[:, part], new_hbm.at[:, part], store_sem.at[c])

    copies[0].wait()
    copies[1].wait()

    @pl.loop(0, ROWS // wide)
    def _(c):
        tall = jnp.concatenate(
            [rows[pl.ds(c * wide + w, COLS, stride=ROWS), :] for w in range(wide)], axis=1
        )
        hi, lo = split(tall)
        result = dot(left[:, 0 : 3 * COLS], jnp.concatenate([hi, hi, lo], axis=0), 1, 0)
        for w in range(wide):
            made[pl.ds(c * wide + w, COLS, stride=ROWS), :] = result[:, w * ZC : (w + 1) * ZC]
        store(c).start()

    @pl.loop(0, ROWS // wide)
    def _(c):
        store(c).wait()

    copies[2].wait()


def on_device(nx, ny, pops, rate, mask, sv, basis, snaps):
    sv = sv.reshape(1, RANK)
    basis = basis.reshape(RANK, ROWS, ZC)
    snaps = snaps.reshape(OLD, ROWS, ZC)
    anywhere = pl.BlockSpec(memory_space=pl.ANY)
    here = pl.BlockSpec(memory_space=pltpu.VMEM)
    owners = COLS // 8

    def f32(*shape):
        return jax.ShapeDtypeStruct(shape, F32)

    def vmem(*shape):
        return pltpu.VMEM(shape, F32)

    dma = pltpu.SemaphoreType.DMA
    field, coarse, inverse, upper, border = pl.pallas_call(
        functools.partial(main_kernel, nx, ny),
        out_shape=(
            f32(19, NX, NY, NZ),
            f32(ROWS, ZC),
            f32(COLS, ZC),
            f32(COLS, ZC),
            f32(8, ZC),
        ),
        in_specs=[anywhere, anywhere, anywhere, here, anywhere, anywhere],
        out_specs=(anywhere, here, here, here, here),
        scratch_shapes=[
            vmem(19, NX, NY, NZ),
            vmem(NX, NY, NZ),
            pltpu.VMEM((NX, NY, NZ), jnp.int32),
            vmem(COLS, ROWS, ZC),
            vmem(19, NX + 2, NY, NZ),
            vmem(19, NX + 2, NY, NZ),
            vmem(2, 5, NX, NZ),
            vmem(2, 5, NX, NZ),
            vmem(2, 5, NX + 16, NZ),
            vmem(2, 5, NX + 16, NZ),
            vmem(2, 4, NY, NZ),
            vmem(3 * XC * NY, NZ),
            vmem(3 * XC * NY, ZC),
            vmem(2 * COLS, ZC),
            vmem(COLS, ZC),
            vmem(nx, 8, ZC),
            vmem(2, 8, ZC),
            vmem(ny, 8, ZC),
            vmem(owners, 8, ZC),
            vmem(ZC, ZC),
            vmem(2, 8, ZC),
            vmem(nx, 8, ZC),
            vmem(ny, 8, ZC),
            vmem(8, ZC),
            dma((NX,)),
            dma((4,)),
            dma((NX,)),
            dma((2, 8)),
            dma((2, 8)),
            dma((5,)),
            dma((5,)),
        ],
        compiler_params=pltpu.CompilerParams(
            collective_id=0, has_side_effects=True, vmem_limit_bytes=40 * 2**20
        ),
        name="substeps",
    )(pops, rate, mask, sv, basis, snaps)
    out, factor, fresh = pl.pallas_call(
        finish_kernel,
        out_shape=(f32(19, NX, NY, NZ), f32(COLS, COLS), f32(COLS, ROWS, ZC)),
        in_specs=[anywhere, here, anywhere, anywhere, here, here, here, here],
        out_specs=(anywhere, here, anywhere),
        scratch_shapes=[
            vmem(COLS, ROWS, ZC),
            vmem(COLS, ROWS, ZC),
            pltpu.VMEM((COLS, 2 * ZC), BF16),
            vmem(8, ZC),
            dma((3,)),
            dma((ROWS // 8,)),
        ],
        compiler_params=pltpu.CompilerParams(vmem_limit_bytes=40 * 2**20),
        name="finish",
    )(field, sv, basis, snaps, coarse, inverse, upper, border)
    return out, factor, fresh.reshape(COLS, 3, XC, YC, ZC)


def solution(mesh):
    return jax.shard_map(
        functools.partial(on_device, mesh.shape["gx"], mesh.shape["gy"]),
        mesh=mesh,
        in_specs=(
            P(None, "gx", "gy", None),
            P("gx", "gy", None),
            P("gx", "gy", None),
            P(),
            P(None, None, "gx", "gy", None),
            P(None, None, "gx", "gy", None),
        ),
        out_specs=(P(None, "gx", "gy", None), P(), P(None, None, "gx", "gy", None)),
        check_vma=False,
    )
```

profile of v0, /device:TPU:1, one launch (start us, length us, event | category | flops | bytes accessed | tf_op | source)
XLA Modules:
  0.0 61.4 jit_solution(13396951622039140421)
XLA Ops:
  0.6 0.0 copy-start
  0.6 1.9 %copy-done = f32[64,3,8,4,128]{4,3,2,1,0:T(4,128)S(1)} copy-done((f32[64,3,8,4,128]{4,3,2,1,0:T(4,128)S(1)}, f32[64,3,8,4,128]{4,3,2,1,0:T(4,128)}, u32[]{:S(2)}) %copy-start) | copy-done | bytes 3145752
  2.5 0.0 copy-start.2
  2.5 1.1 %copy-done.2 = f32[15,3,8,4,128]{4,3,2,1,0:T(4,128)S(1)} copy-done((f32[15,3,8,4,128]{4,3,2,1,0:T(4,128)S(1)}, f32[15,3,8,4,128]{4,3,2,1,0:T(4,128)}, u32[]{:S(2)}) %copy-start.2) | copy-done | bytes 737304
  3.6 0.0 copy-start.4
  3.6 1.7 %copy-done.4 = f32[19,16,8,256]{3,2,1,0:T(8,128)S(1)} copy-done((f32[19,16,8,256]{3,2,1,0:T(8,128)S(1)}, f32[19,16,8,256]{3,2,1,0:T(8,128)}, u32[]{:S(2)}) %copy-start.4) | copy-done | bytes 2490392
  5.3 0.0 copy-start.5
  5.3 0.9 %copy-done.5 = f32[16,8,256]{2,1,0:T(8,128)S(1)} copy-done((f32[16,8,256]{2,1,0:T(8,128)S(1)}, f32[16,8,256]{2,1,0:T(8,128)}, u32[]{:S(2)}) %copy-start.5) | copy-done | bytes 131096
  6.2 0.0 copy-start.6
  6.2 0.9 %copy-done.6 = s32[16,8,256]{2,1,0:T(8,128)S(1)} copy-done((s32[16,8,256]{2,1,0:T(8,128)S(1)}, s32[16,8,256]{2,1,0:T(8,128)}, u32[]{:S(2)}) %copy-start.6) | copy-done | bytes 131096
  7.2 0.0 copy-start.7
  7.2 0.7 %copy-done.7 = f32[64]{0:T(128)S(1)} copy-done((f32[64]{0:T(128)S(1)}, f32[64]{0:T(128)}, u32[]{:S(2)}) %copy-start.7) | copy-done | bytes 280
  7.8 0.0 copy-start.1
  7.8 0.0 copy-start.3
  7.8 45.5 %substeps.1 = (f32[19,16,8,256]{3,2,1,0:T(8,128)S(1)}, f32[96,128]{1,0:T(8,128)S(1)}, f32[80,128]{1,0:T(8,128)S(1)}, f32[80,128]{1,0:T(8,128)S(1)}, f32[8,128]{1,0:T(8,128)S(1)}) custom-call(f32[19,16,8,256]{3,2,1,0:T(8,128)S(1)} %copy-done.4, f32[16,8,256]{2,1,0:T(8,128)S(1)} %copy-done.5, s32[16,8,256]{2,1,0:T(8,128)S(1)} %copy-done.6, ...), custom_call_target="tpu_custom_call" | custom-call | tf_op jit(solution)/shard_map/substeps/pallas_call | solution.py:614
  53.3 0.0 copy-done.1
  53.3 0.0 copy-done.3
  53.3 8.1 %finish.1 = (f32[19,16,8,256]{3,2,1,0:T(8,128)}, f32[80,80]{1,0:T(8,128)}, f32[80,96,128]{2,1,0:T(8,128)}) custom-call(f32[19,16,8,256]{3,2,1,0:T(8,128)S(1)} %get-tuple-element.11.field_hbm, f32[1,64]{1,0:T(1,128)S(1)} %bitcast.9, f32[64,96,128]{2,1,0:T(8,128)S(1)} %bitcast.5, f32[15,96,128]{2,1,0:T(8,128)S(1)} %bitcast.7, ...), custom_call_target="tpu_custom_call" | custom-call | tf_op jit(solution)/shard_map/finish/pallas_call | solution.py:663
Async XLA Ops:
  0.6 1.9 %copy-start = (f32[64,3,8,4,128]{4,3,2,1,0:T(4,128)S(1)}, f32[64,3,8,4,128]{4,3,2,1,0:T(4,128)}, u32[]{:S(2)}) copy-start(f32[64,3,8,4,128]{4,3,2,1,0:T(4,128)} %param.10) | copy-start | bytes 9437188
  2.5 1.1 %copy-start.2 = (f32[15,3,8,4,128]{4,3,2,1,0:T(4,128)S(1)}, f32[15,3,8,4,128]{4,3,2,1,0:T(4,128)}, u32[]{:S(2)}) copy-start(f32[15,3,8,4,128]{4,3,2,1,0:T(4,128)} %param.11) | copy-start | bytes 2211844
  3.6 1.7 %copy-start.4 = (f32[19,16,8,256]{3,2,1,0:T(8,128)S(1)}, f32[19,16,8,256]{3,2,1,0:T(8,128)}, u32[]{:S(2)}) copy-start(f32[19,16,8,256]{3,2,1,0:T(8,128)} %pops_hbm.1) | copy-start | bytes 7471108
  5.3 0.9 %copy-start.5 = (f32[16,8,256]{2,1,0:T(8,128)S(1)}, f32[16,8,256]{2,1,0:T(8,128)}, u32[]{:S(2)}) copy-start(f32[16,8,256]{2,1,0:T(8,128)} %rate_hbm.1) | copy-start | bytes 393220
  6.2 0.9 %copy-start.6 = (s32[16,8,256]{2,1,0:T(8,128)S(1)}, s32[16,8,256]{2,1,0:T(8,128)}, u32[]{:S(2)}) copy-start(s32[16,8,256]{2,1,0:T(8,128)} %mask_hbm.1) | copy-start | bytes 393220
  7.2 0.7 %copy-start.7 = (f32[64]{0:T(128)S(1)}, f32[64]{0:T(128)}, u32[]{:S(2)}) copy-start(f32[64]{0:T(128)} %param.9) | copy-start | bytes 772
  7.8 45.5 %copy-start.1 = (f32[64,3,8,4,128]{4,3,2,1,0:T(4,128)S(1)}, f32[64,3,8,4,128]{4,3,2,1,0:T(4,128)}, u32[]{:S(2)}) copy-start(f32[64,3,8,4,128]{4,3,2,1,0:T(4,128)} %param.10) | copy-start | bytes 9437188
  7.8 45.5 %copy-start.3 = (f32[15,3,8,4,128]{4,3,2,1,0:T(4,128)S(1)}, f32[15,3,8,4,128]{4,3,2,1,0:T(4,128)}, u32[]{:S(2)}) copy-start(f32[15,3,8,4,128]{4,3,2,1,0:T(4,128)} %param.11) | copy-start | bytes 2211844
where the time goes:
time: 61.7 us; the launch traced here: 61.4 us
  Pallas kernels  53.6 us (87%)
  local copies, waits for them, and re-layouts  7.17 us (12%)
  between operations  0.67 us (1%)
    pallas_call x1, Pallas kernels, on_device(): pl.pallas_call(functools.partial(main_kernel, nx, ny), out_shape=(f32(19,...  45.5 us
    pallas_call x1, Pallas kernels, on_device(): pl.pallas_call(finish_kernel, out_shape=(f32(19, NX, NY, NZ), f32(COLS, C...  8.11 us
    unnamed x16, local copies, waits for them, and re-layouts  7.17 us

commit v1 on v0

--- a/solution.py
+++ b/solution.py
@@ -45,6 +45,7 @@
 XC, YC, ZC = 8, 4, 128
 COLS, RANK, OLD = 80, 64, 15
 ROWS = 3 * XC * YC
+PITCH = ROWS + 8
 HALO0 = 8
 
 
@@ -125,10 +126,55 @@
     )
 
 
-def scale_row(ref, sv_ref):
-    ref[...] = jnp.ones_like(ref)
-    ref[0:1, 0:RANK] = sv_ref[...]
-    return ref[0:1, :]
+def split3(x):
+    hi = x.astype(BF16).astype(F32)
+    mid = (x - hi).astype(BF16).astype(F32)
+    return hi, mid, x - hi - mid
+
+
+def outer8(r, t):
+    h, m, l = split3(jnp.concatenate([r, t], axis=1))
+    rh, rm, rl = h[:, 0:ZC], m[:, 0:ZC], l[:, 0:ZC]
+    a = jnp.concatenate([rh, rh, rh, rm, rm, rl], axis=0).astype(BF16)
+    b = jnp.concatenate([h, m, l, h, m, h], axis=0).astype(BF16)
+    return dot(a, b, 0, 0)
+
+
+def eliminate(rows, extra, first):
+    d = [
+        [jnp.broadcast_to(rows[i][:, first + j : first + j + 1], (1, ZC)) for j in range(i + 1)]
+        for i in range(8)
+    ]
+    r, t = list(rows), list(extra)
+    for j in range(8):
+        inv = lax.rsqrt(d[j][j])
+        r[j] = r[j] * inv
+        t[j] = t[j] * inv
+        col = [None if i <= j else d[i][j] * inv for i in range(8)]
+        for i in range(j + 1, 8):
+            for k in range(j + 1, i + 1):
+                d[i][k] = d[i][k] - col[i] * col[k]
+            r[i] = r[i] - col[i] * r[j]
+            t[i] = t[i] - col[i] * t[j]
+    return jnp.concatenate(r, axis=0), jnp.concatenate(t, axis=0)
+
+
+def factor_block(b, work, inverse, upper):
+    row8 = lax.broadcasted_iota(jnp.int32, (8, ZC), 0)
+    lane8 = lax.broadcasted_iota(jnp.int32, (8, ZC), 1)
+    o = 8 * b
+    r, t = eliminate(
+        [work[o + i : o + i + 1, :] for i in range(8)],
+        [inverse[o + i : o + i + 1, :] for i in range(8)],
+        o,
+    )
+    r = jnp.where(lane8 >= row8 + o, r, 0.0)
+    upper[o : o + 8, :] = r
+    inverse[o : o + 8, :] = t
+    if o + 8 < COLS:
+        change = outer8(r, t)
+        work[o + 8 : COLS, :] = work[o + 8 : COLS, :] - change[o + 8 : COLS, 0:ZC]
+        inverse[o + 8 : COLS, :] = inverse[o + 8 : COLS, :] - change[o + 8 : COLS, ZC:]
 
 
 def main_kernel(
@@ -137,10 +183,11 @@
     pops_hbm,
     rate_hbm,
     mask_hbm,
-    sv_ref,
+    sv_hbm,
     basis_hbm,
     snaps_hbm,
-    field_hbm,
+    field_out,
+    fresh,
     coarse_ref,
     inverse_ref,
     upper_ref,
@@ -164,14 +211,16 @@
     send_b,
     recv_b,
     recv_c,
-    vec_a,
+    sums8,
     vec_b,
     vec_in_a,
     vec_in_b,
+    sv,
     scale,
+    work,
+    left,
     plane_sem,
     load_sem,
-    store_sem,
     halo_send,
     halo_recv,
     red_send,
@@ -190,18 +239,21 @@
     loads = [
         pltpu.make_async_copy(rate_hbm, rate, load_sem.at[0]),
         pltpu.make_async_copy(mask_hbm, mask, load_sem.at[1]),
-        pltpu.make_async_copy(basis_hbm, stack.at[pl.ds(0, RANK)], load_sem.at[2]),
-        pltpu.make_async_copy(snaps_hbm, stack.at[pl.ds(RANK, OLD)], load_sem.at[3]),
+        pltpu.make_async_copy(basis_hbm, stack.at[pl.ds(0, RANK), pl.ds(0, ROWS)], load_sem.at[2]),
+        pltpu.make_async_copy(snaps_hbm, stack.at[pl.ds(RANK, OLD), pl.ds(0, ROWS)], load_sem.at[3]),
+        pltpu.make_async_copy(sv_hbm, sv, load_sem.at[4]),
     ]
-    loads[0].start()
-    loads[1].start()
 
     @pl.loop(0, NX)
     def _(x):
         load_plane(x).start()
 
+    loads[0].start()
+    loads[1].start()
+
     loads[2].start()
     loads[3].start()
+    loads[4].start()
 
     barrier = pltpu.get_barrier_semaphore()
 
@@ -221,7 +273,8 @@
         for dy in (-1, 1):
             pl.semaphore_signal(barrier, inc=1, device_id=shifted(dx, dy), device_id_type=MESH)
 
-    stack[COLS - 1] = jnp.zeros((ROWS, ZC), F32)
+    stack[COLS - 1] = jnp.zeros((PITCH, ZC), F32)
+    scale[...] = jnp.ones_like(scale)
 
     def put(post, step, x):
         for i in range(19):
@@ -278,19 +331,20 @@
 
     loads[2].wait()
     loads[3].wait()
-    rows = stack.reshape(COLS * ROWS, ZC)
+    loads[4].wait()
+    rows = stack.reshape(COLS * PITCH, ZC)
     gram[...] = jnp.zeros_like(gram)
-    wide = 8
-
-    @pl.loop(0, ROWS // wide)
+
+    def tall(c, wide):
+        return jnp.concatenate(
+            [rows[pl.ds(c * wide + w, COLS, stride=PITCH), :] for w in range(wide)], axis=1
+        )
+
+    @pl.loop(0, ROWS // 32)
     def _(c):
-        tall = jnp.concatenate(
-            [rows[pl.ds(c * wide + w, COLS, stride=ROWS), :] for w in range(wide)], axis=1
-        )
-        hi, lo = split(tall)
+        hi, lo = split(tall(c, 32))
         gram[:, 0:COLS] += dot(jnp.concatenate([hi, lo], axis=0), hi, 1, 1)
 
-    parts[0:COLS, :] = gram[0:COLS, :]
     low = jnp.concatenate([gram[COLS : 2 * COLS, :], jnp.zeros((ZC - COLS, ZC), F32)], axis=0)
     parts[...] = gram[0:COLS, :] + low[0:COLS] + jnp.transpose(low)[0:COLS]
 
@@ -374,10 +428,16 @@
 
     for copy in second:
         copy.wait_recv()
+
+    @pl.when(mx < owners)
+    def _():
+        wait_for(recv_b.at[pl.ds(0, ny - 1)], red_recv.at[1])
+        value = total(recv_b, ny)
+        send_b[1] = value
+        recv_c[mx] = value
+        start_all(ring_c, nx)
+
     land(1)
-
-    def store_plane(x):
-        return pltpu.make_async_copy(pops.at[:, x], field_hbm.at[:, x], store_sem.at[x])
 
     @pl.loop(0, XC)
     def _(xc):
@@ -386,8 +446,7 @@
             x = 2 * xc + half
             field = arrive(post_b, in_up.at[1], in_down.at[1], x)
             for i in range(19):
-                pops[i, x] = field[i]
-            store_plane(x).start()
+                field_out[i, x] = field[i]
             fluid = mask[x] == 0
             for a, u in enumerate(flow(field)[1]):
                 u = jnp.where(fluid, u, 0.0)
@@ -395,36 +454,32 @@
         for a in range(3):
             vel[pl.ds(pl.multiple_of(a * XC * NY + xc * NY, NY), NY), :] = sums[a]
 
-    @pl.when(mx < owners)
-    def _():
-        wait_for(recv_b.at[pl.ds(0, ny - 1)], red_recv.at[1])
-        value = total(recv_b, ny)
-        send_b[1] = value
-        recv_c[mx] = value
-        start_all(ring_c, nx)
-
     fine = lax.broadcasted_iota(jnp.int32, (NZ, ZC), 0)
     pair = lax.broadcasted_iota(jnp.int32, (NZ, ZC), 1)
     pick = jnp.where(fine // 2 == pair, SPEED_SCALE / 8.0, 0.0).astype(F32)
     pooled[...] = dot(vel[...], pick, 1, 0, HIGHEST)
     coarse = pooled[pl.ds(0, ROWS, stride=2), :] + pooled[pl.ds(1, ROWS, stride=2), :]
     coarse_ref[...] = coarse
-    stack[COLS - 1] = coarse
-
-    vec_a[...] = jnp.zeros_like(vec_a)
-
-    @pl.loop(0, ROWS // wide)
-    def _(c):
-        value = vec_a[0:COLS, :]
-        for w in range(wide):
-            r = c * wide + w
-            value = value + rows[pl.ds(r, COLS, stride=ROWS), :] * coarse_ref[pl.ds(r, 1), :]
-        vec_a[0:COLS, :] = value
-
-    last = dot(jnp.ones((8, ZC), F32), vec_a[...], 1, 1, HIGHEST)
+    stack[COLS - 1, 0:ROWS, :] = coarse
+
+    tiles = ROWS // 8
+    parted = coarse.reshape(tiles, 8, ZC)
+
+    @pl.loop(0, COLS // 8)
+    def _(k):
+        for q in range(8):
+            column = stack[k * 8 + q, 0:ROWS, :].reshape(tiles, 8, ZC)
+            sums8[pl.ds(pl.multiple_of(k * 64 + q * 8, 8), 8), :] = jnp.sum(column * parted, axis=0)
+
+    folded = sums8[pl.ds(0, COLS, stride=8), :]
+    for q in range(1, 8):
+        folded = folded + sums8[pl.ds(q, COLS, stride=8), :]
+    folded = jnp.concatenate([folded, jnp.zeros((ZC - COLS, ZC), F32)], axis=0)
+    last = dot(jnp.ones((8, ZC), F32), folded, 1, 1, HIGHEST)
+    one = pl.ds(0, 1)
     vec_b[0] = last
     vec_in_a[mx] = last
-    ring_d = all_along(vec_b.at[0], vec_in_a.at[mx], 3, 0)
+    ring_d = all_along(vec_b.at[0, one], vec_in_a.at[mx, one], 3, 0)
     start_all(ring_d, nx)
 
     @pl.when(mx < owners)
@@ -437,56 +492,55 @@
 
     row = lax.broadcasted_iota(jnp.int32, (COLS, ZC), 0)
     lane = lax.broadcasted_iota(jnp.int32, (COLS, ZC), 1)
-    srow = scale_row(scale, sv_ref)
+    scale[0:1, 0:RANK] = sv[...]
+    srow = scale[0:1, :]
     scol = jnp.sum(jnp.where(row == lane, srow, 0.0), axis=1, keepdims=True)
     per_row = 1.0 / (all_rows(nx, ny))
     whole = jnp.concatenate([recv_c[c] for c in range(owners)], axis=0)
     whole = whole * (srow * scol) * per_row
     whole = jnp.where((row == COLS - 1) & (lane == COLS - 1), 1.0, whole)
 
-    row8 = lax.broadcasted_iota(jnp.int32, (8, ZC), 0)
-    lane8 = lax.broadcasted_iota(jnp.int32, (8, ZC), 1)
-
-    def eight(b, state):
-        a, e = state
-        r, t = a[0:8], e[0:8]
-        for j in range(8):
-            pivot = r[j : j + 1, j : j + 1]
-            inv = lax.rsqrt(pivot)
-            inv = inv * (1.5 - 0.5 * pivot * inv * inv)
-            factor = jnp.where(row8[:, 0:1] > j, r[:, j : j + 1] * inv, 0.0)
-            urow, trow = r[j : j + 1] * inv, t[j : j + 1] * inv
-            r = jnp.where(row8 == j, urow, r - factor * urow)
-            t = jnp.where(row8 == j, trow, t - factor * trow)
-        r = jnp.where((lane8 >= row8) & (lane8 < COLS - 8 * b), r, 0.0)
-        at = pl.ds(pl.multiple_of(8 * b, 8), 8)
-        upper_ref[at, :] = pltpu.roll(r, 8 * b, axis=1)
-        inverse_ref[at, :] = t
-        change = dot(r, jnp.concatenate([r, t], axis=1), 0, 0, HIGHEST)
-        zero = jnp.zeros((8, ZC), F32)
-        a = jnp.concatenate([a[8:] - change[8:COLS, 0:ZC], zero], axis=0)
-        e = jnp.concatenate([e[8:] - change[8:COLS, ZC:], zero], axis=0)
-        return pltpu.roll(a, ZC - 8, axis=1), e
-
-    state = (whole, (row == lane).astype(F32))
-    half = (owners + 1) // 2
-    state = lax.fori_loop(0, half, eight, state)
-
-    wait_for(vec_in_a.at[pl.ds(0, nx - 1)], red_recv.at[3])
-    value = total(vec_in_a, nx)
+    work[...] = whole
+    inverse_ref[...] = (row == lane).astype(F32)
+
+    def vec_total(ref, count):
+        value = ref[0, 0:1, :]
+        for j in range(1, count):
+            value = value + ref[j, 0:1, :]
+        return value
+
+    half = owners // 2 - 1
+    for b in range(half):
+        factor_block(b, work, inverse_ref, upper_ref)
+
+    wait_for(vec_in_a.at[pl.ds(0, nx - 1), one], red_recv.at[3])
+    value = jnp.broadcast_to(vec_total(vec_in_a, nx), (8, ZC))
     vec_b[1] = value
     vec_in_b[my] = value
-    ring_e = all_along(vec_b.at[1], vec_in_b.at[my], 4, 1)
+    ring_e = all_along(vec_b.at[1, one], vec_in_b.at[my, one], 4, 1)
     start_all(ring_e, ny)
 
-    lax.fori_loop(half, owners, eight, state)
-
-    wait_for(vec_in_b.at[pl.ds(0, ny - 1)], red_recv.at[4])
-    border_ref[...] = total(vec_in_b, ny) * srow * per_row
-
-    @pl.loop(0, NX)
-    def _(x):
-        store_plane(x).wait()
+    for b in range(half, owners):
+        factor_block(b, work, inverse_ref, upper_ref)
+
+    scaled = inverse_ref[...] * srow
+    hi = scaled.astype(BF16).astype(F32)
+    lo = scaled - hi
+    none = jnp.zeros_like(hi)
+    hi, lo = jnp.concatenate([hi, none], axis=1), jnp.concatenate([lo, none], axis=1)
+    placed = hi + pltpu.roll(lo, COLS, axis=1) + pltpu.roll(hi, 2 * COLS, axis=1)
+    left[...] = placed.astype(BF16)
+    made = fresh.reshape(COLS * PITCH, ZC)
+
+    @pl.loop(0, ROWS // 16)
+    def _(c):
+        hi, lo = split(tall(c, 16))
+        result = dot(left[:, 0 : 3 * COLS], jnp.concatenate([hi, hi, lo], axis=0), 1, 0)
+        for w in range(16):
+            made[pl.ds(c * 16 + w, COLS, stride=PITCH), :] = result[:, w * ZC : (w + 1) * ZC]
+
+    wait_for(vec_in_b.at[pl.ds(0, ny - 1), one], red_recv.at[4])
+    border_ref[...] = jnp.broadcast_to(vec_total(vec_in_b, ny) * srow * per_row, (8, ZC))
 
     for copy in first + second:
         copy.wait_send()
@@ -501,8 +555,8 @@
     def _():
         wait_for(recv_a.at[pl.ds(0, owners)], red_send.at[0])
 
-    wait_for(vec_in_a.at[pl.ds(0, nx - 1)], red_send.at[3])
-    wait_for(vec_in_b.at[pl.ds(0, ny - 1)], red_send.at[4])
+    wait_for(vec_in_a.at[pl.ds(0, nx - 1), one], red_send.at[3])
+    wait_for(vec_in_b.at[pl.ds(0, ny - 1), one], red_send.at[4])
 
 
 def all_rows(nx, ny):
@@ -510,10 +564,8 @@
 
 
 def finish_kernel(
-    field_hbm,
-    sv_ref,
-    basis_hbm,
-    snaps_hbm,
+    field_ref,
+    fresh_ref,
     coarse_ref,
     inverse_ref,
     upper_ref,
@@ -521,22 +573,18 @@
     pops_hbm,
     factor_ref,
     new_hbm,
-    stack,
-    fresh,
-    left,
-    scale,
-    load_sem,
-    store_sem,
+    column,
+    newest,
+    sem,
 ):
-    wide = 8
+    done = pl.ds(0, COLS - 1)
     copies = [
-        pltpu.make_async_copy(basis_hbm, stack.at[pl.ds(0, RANK)], load_sem.at[0]),
-        pltpu.make_async_copy(snaps_hbm, stack.at[pl.ds(RANK, OLD)], load_sem.at[1]),
-        pltpu.make_async_copy(field_hbm, pops_hbm, load_sem.at[2]),
+        pltpu.make_async_copy(fresh_ref.at[done, pl.ds(0, ROWS)], new_hbm.at[done], sem.at[0]),
+        pltpu.make_async_copy(field_ref, pops_hbm, sem.at[1]),
+        pltpu.make_async_copy(newest, new_hbm.at[COLS - 1], sem.at[2]),
     ]
-    for copy in copies:
-        copy.start()
-    stack[COLS - 1] = coarse_ref[...]
+    copies[0].start()
+    copies[1].start()
 
     row = lax.broadcasted_iota(jnp.int32, (COLS, ZC), 0)
     lane = lax.broadcasted_iota(jnp.int32, (COLS, ZC), 1)
@@ -544,63 +592,33 @@
     border = border_ref[...]
     lane8 = lax.broadcasted_iota(jnp.int32, (8, ZC), 1)
     old = jnp.where(lane8 < COLS - 1, border, 0.0)
-    tall = jnp.concatenate([inverse, jnp.zeros((ZC - COLS, ZC), F32)], axis=0)
-    lrow = dot(old, tall, 1, 1, HIGHEST)
-    lrow = jnp.where(lane8 < COLS - 1, lrow, 0.0)
-    wide_old = jnp.concatenate([old] * (ZC // 8), axis=0)
-    lcol = dot(inverse, wide_old, 1, 1, HIGHEST)
-    left_over = border[0:1, COLS - 1 : COLS] - jnp.sum(lrow[0:1] * lrow[0:1], axis=1, keepdims=True)
-    inv = lax.rsqrt(left_over)
-    inv = inv * (1.5 - 0.5 * left_over * inv * inv)
-    diag = left_over * inv
-    end = dot(lrow, tall, 1, 0, HIGHEST)[0:1]
-    end = jnp.where(lane[0:1] == COLS - 1, inv, -end * inv)
-    inverse = jnp.where(row == COLS - 1, end, inverse)
-    final = jnp.where(lane == COLS - 1, jnp.where(row == COLS - 1, diag, lcol), upper_ref[...])
-    final = jnp.where((row == COLS - 1) & (lane < COLS - 1), 0.0, final)
-    factor_ref[...] = final[:, 0:COLS]
-
-    inverse = inverse * scale_row(scale, sv_ref)
-    hi = inverse.astype(BF16).astype(F32)
-    lo = inverse - hi
-    none = jnp.zeros_like(hi)
-    hi, lo = jnp.concatenate([hi, none], axis=1), jnp.concatenate([lo, none], axis=1)
-    placed = hi + pltpu.roll(lo, COLS, axis=1) + pltpu.roll(hi, 2 * COLS, axis=1)
-    left[...] = placed.astype(BF16)
-
-    rows = stack.reshape(COLS * ROWS, ZC)
-    made = fresh.reshape(COLS * ROWS, ZC)
-
-    def store(c):
-        part = pl.ds(pl.multiple_of(c * wide, wide), wide)
-        return pltpu.make_async_copy(fresh.at[:, part], new_hbm.at[:, part], store_sem.at[c])
-
-    copies[0].wait()
-    copies[1].wait()
-
-    @pl.loop(0, ROWS // wide)
-    def _(c):
-        tall = jnp.concatenate(
-            [rows[pl.ds(c * wide + w, COLS, stride=ROWS), :] for w in range(wide)], axis=1
-        )
-        hi, lo = split(tall)
-        result = dot(left[:, 0 : 3 * COLS], jnp.concatenate([hi, hi, lo], axis=0), 1, 0)
-        for w in range(wide):
-            made[pl.ds(c * wide + w, COLS, stride=ROWS), :] = result[:, w * ZC : (w + 1) * ZC]
-        store(c).start()
-
-    @pl.loop(0, ROWS // wide)
-    def _(c):
-        store(c).wait()
-
-    copies[2].wait()
+    lcol = dot(inverse, jnp.concatenate([old] * (ZC // 8), axis=0), 1, 1, HIGHEST)
+    lcol = jnp.where(row < COLS - 1, lcol, 0.0)
+    column[...] = lcol
+    square = border[0:1, COLS - 1 : COLS] - jnp.sum(lcol * lcol, axis=0, keepdims=True)
+    inv = lax.rsqrt(square)
+    end = jnp.where(row == COLS - 1, square * inv, lcol)
+    factor_ref[...] = jnp.where(lane == COLS - 1, end, upper_ref[...])[:, 0:COLS]
+
+    def minus(k, value):
+        for q in range(8):
+            i = k * 8 + q
+            value = value - column[pl.ds(i, 1), :] * fresh_ref[i, 0:ROWS, :]
+        return value
+
+    newest[...] = lax.fori_loop(0, COLS // 8, minus, coarse_ref[...]) * inv
+    copies[2].start()
+    for copy in copies:
+        copy.wait()
 
 
 def on_device(nx, ny, pops, rate, mask, sv, basis, snaps):
     sv = sv.reshape(1, RANK)
     basis = basis.reshape(RANK, ROWS, ZC)
     snaps = snaps.reshape(OLD, ROWS, ZC)
-    anywhere = pl.BlockSpec(memory_space=pl.ANY)
+    given = (pops, rate, mask, sv, basis, snaps)
+    given = [pltpu.with_memory_space_constraint(x, pltpu.HBM) for x in given]
+    far = pl.BlockSpec(memory_space=pltpu.HBM)
     here = pl.BlockSpec(memory_space=pltpu.VMEM)
     owners = COLS // 8
 
@@ -611,22 +629,23 @@
         return pltpu.VMEM(shape, F32)
 
     dma = pltpu.SemaphoreType.DMA
-    field, coarse, inverse, upper, border = pl.pallas_call(
+    field, fresh, coarse, inverse, upper, border = pl.pallas_call(
         functools.partial(main_kernel, nx, ny),
         out_shape=(
             f32(19, NX, NY, NZ),
+            f32(COLS, PITCH, ZC),
             f32(ROWS, ZC),
             f32(COLS, ZC),
             f32(COLS, ZC),
             f32(8, ZC),
         ),
-        in_specs=[anywhere, anywhere, anywhere, here, anywhere, anywhere],
-        out_specs=(anywhere, here, here, here, here),
+        in_specs=[far] * 6,
+        out_specs=(here,) * 6,
         scratch_shapes=[
             vmem(19, NX, NY, NZ),
             vmem(NX, NY, NZ),
             pltpu.VMEM((NX, NY, NZ), jnp.int32),
-            vmem(COLS, ROWS, ZC),
+            vmem(COLS, PITCH, ZC),
             vmem(19, NX + 2, NY, NZ),
             vmem(19, NX + 2, NY, NZ),
             vmem(2, 5, NX, NZ),
@@ -642,14 +661,16 @@
             vmem(2, 8, ZC),
             vmem(ny, 8, ZC),
             vmem(owners, 8, ZC),
-            vmem(ZC, ZC),
+            vmem(8 * COLS, ZC),
             vmem(2, 8, ZC),
             vmem(nx, 8, ZC),
             vmem(ny, 8, ZC),
+            vmem(1, RANK),
             vmem(8, ZC),
+            vmem(COLS, ZC),
+            pltpu.VMEM((COLS, 2 * ZC), BF16),
             dma((NX,)),
-            dma((4,)),
-            dma((NX,)),
+            dma((5,)),
             dma((2, 8)),
             dma((2, 8)),
             dma((5,)),
@@ -659,24 +680,17 @@
             collective_id=0, has_side_effects=True, vmem_limit_bytes=40 * 2**20
         ),
         name="substeps",
-    )(pops, rate, mask, sv, basis, snaps)
-    out, factor, fresh = pl.pallas_call(
+    )(*given)
+    out, factor, new = pl.pallas_call(
         finish_kernel,
         out_shape=(f32(19, NX, NY, NZ), f32(COLS, COLS), f32(COLS, ROWS, ZC)),
-        in_specs=[anywhere, here, anywhere, anywhere, here, here, here, here],
-        out_specs=(anywhere, here, anywhere),
-        scratch_shapes=[
-            vmem(COLS, ROWS, ZC),
-            vmem(COLS, ROWS, ZC),
-            pltpu.VMEM((COLS, 2 * ZC), BF16),
-            vmem(8, ZC),
-            dma((3,)),
-            dma((ROWS // 8,)),
-        ],
-        compiler_params=pltpu.CompilerParams(vmem_limit_bytes=40 * 2**20),
+        in_specs=[here] * 6,
+        out_specs=(far, here, far),
+        scratch_shapes=[vmem(COLS, ZC), vmem(ROWS, ZC), dma((3,))],
+        compiler_params=pltpu.CompilerParams(vmem_limit_bytes=16 * 2**20),
         name="finish",
-    )(field, sv, basis, snaps, coarse, inverse, upper, border)
-    return out, factor, fresh.reshape(COLS, 3, XC, YC, ZC)
+    )(field, fresh, coarse, inverse, upper, border)
+    return out, factor, new.reshape(COLS, 3, XC, YC, ZC)
 
 
 def solution(mesh):

time: 61.7 us -> 41.5 us (0.67)
  Pallas kernels: 53.6 us -> 40.7 us
  local copies, waits for them, and re-layouts: 7.17 us -> 0 us
    pallas_call x1, Pallas kernels: 45.5 us -> 37.4 us  [on_device(): pl.pallas_call(functools.partial(main_kernel, nx, ny), out_shape=(f32(19,...]
    unnamed x16 -> x0, local copies, waits for them, and re-layouts: 7.17 us -> none
    pallas_call x1, Pallas kernels: 8.11 us -> 3.38 us  [on_device(): pl.pallas_call(finish_kernel, out_shape=(f32(19, NX, NY, NZ), f32(COLS, C...]
where the time goes in v1:
time: 41.5 us; the launch traced here: 41.4 us
  Pallas kernels  40.7 us (98%)
  between operations  0.64 us (2%)
    pallas_call x1, Pallas kernels, on_device(): pl.pallas_call(functools.partial(main_kernel, nx, ny), out_shape=(f32(19,...  37.4 us
    pallas_call x1, Pallas kernels, on_device(): pl.pallas_call(finish_kernel, out_shape=(f32(19, NX, NY, NZ), f32(COLS, C...  3.38 us

profile of v1, /device:TPU:1, one launch (start us, length us, event | category | flops | bytes accessed | tf_op | source)
XLA Modules:
  0.0 41.4 jit_solution(15047661686087549184)
XLA Ops:
  0.6 37.4 %substeps.1 = (f32[19,16,8,256]{3,2,1,0:T(8,128)S(1)}, f32[80,104,128]{2,1,0:T(8,128)S(1)}, f32[96,128]{1,0:T(8,128)S(1)}, f32[80,128]{1,0:T(8,128)S(1)}, f32[80,128]{1,0:T(8,128)S(1)}, /*index=5*/f32[8,128]{1,0:T(8,128)S(1)}) custom-call(f32[19,16,8,256]{3,2,1,0:T(8,128)} %pops_hbm.1, f32[16,8,256]{2,1,0:T(8,128)} %rate_hbm.1, s32[16,8,256]{2,1,0:T(8,128)} %mask_hbm.1, ...), custom_call_target="tpu_custom_call" | custom-call | tf_op jit(solution)/shard_map/substeps/pallas_call | solution.py:632
  38.0 3.4 %finish.1 = (f32[19,16,8,256]{3,2,1,0:T(8,128)}, f32[80,80]{1,0:T(8,128)}, f32[80,96,128]{2,1,0:T(8,128)}) custom-call(f32[19,16,8,256]{3,2,1,0:T(8,128)S(1)} %get-tuple-element.12.field_ref, f32[80,104,128]{2,1,0:T(8,128)S(1)} %get-tuple-element.13.fresh_ref, f32[96,128]{1,0:T(8,128)S(1)} %get-tuple-element.14.coarse_ref, ...), custom_call_target="tpu_custom_call" | custom-call | tf_op jit(solution)/shard_map/finish/pallas_call | solution.py:684

commit v2 on v1

--- a/solution.py
+++ b/solution.py
@@ -202,7 +202,6 @@
     out_down,
     in_up,
     in_down,
-    in_corner,
     vel,
     pooled,
     gram,
@@ -233,8 +232,9 @@
     def shifted(dx, dy):
         return (lax.rem(mx + (dx + nx), nx), lax.rem(my + (dy + ny), ny))
 
-    def load_plane(x):
-        return pltpu.make_async_copy(pops_hbm.at[:, x], pops.at[:, x], plane_sem.at[x])
+    def load_planes(g):
+        part = pl.ds(4 * g, 4)
+        return pltpu.make_async_copy(pops_hbm.at[:, part], pops.at[:, part], plane_sem.at[g])
 
     loads = [
         pltpu.make_async_copy(rate_hbm, rate, load_sem.at[0]),
@@ -243,35 +243,31 @@
         pltpu.make_async_copy(snaps_hbm, stack.at[pl.ds(RANK, OLD), pl.ds(0, ROWS)], load_sem.at[3]),
         pltpu.make_async_copy(sv_hbm, sv, load_sem.at[4]),
     ]
-
-    @pl.loop(0, NX)
-    def _(x):
-        load_plane(x).start()
-
+    for g in range(NX // 4):
+        load_planes(g).start()
     loads[0].start()
     loads[1].start()
+
+    barrier = pltpu.get_barrier_semaphore()
+
+    def greet(to):
+        pl.semaphore_signal(barrier, inc=1, device_id=to, device_id_type=MESH)
+
+    for dx in (-1, 1):
+        for dy in (-1, 1):
+            greet(shifted(dx, dy))
+
+    @pl.loop(0, nx - 1)
+    def _(j):
+        greet((lax.rem(mx + nx // 2 + j + lax.div(j, nx // 2), nx), my))
+
+    @pl.loop(0, ny - 1)
+    def _(j):
+        greet((mx, lax.rem(my + ny // 2 + j + lax.div(j, ny // 2), ny)))
 
     loads[2].start()
     loads[3].start()
     loads[4].start()
-
-    barrier = pltpu.get_barrier_semaphore()
-
-    @pl.loop(1, nx)
-    def _(j):
-        pl.semaphore_signal(
-            barrier, inc=1, device_id=(lax.rem(mx + j, nx), my), device_id_type=MESH
-        )
-
-    @pl.loop(1, ny)
-    def _(j):
-        pl.semaphore_signal(
-            barrier, inc=1, device_id=(mx, lax.rem(my + j, ny)), device_id_type=MESH
-        )
-
-    for dx in (-1, 1):
-        for dy in (-1, 1):
-            pl.semaphore_signal(barrier, inc=1, device_id=shifted(dx, dy), device_id_type=MESH)
 
     stack[COLS - 1] = jnp.zeros((PITCH, ZC), F32)
     scale[...] = jnp.ones_like(scale)
@@ -286,15 +282,22 @@
 
     def halo(step):
         post = posts[step]
-        inner = pl.ds(HALO0, NX)
-        moves = [
-            (post.at[pl.ds(0, 5), NX], post.at[pl.ds(0, 5), 0], (1, 0)),
-            (post.at[pl.ds(5, 5), 1], post.at[pl.ds(5, 5), NX + 1], (-1, 0)),
-            (out_up.at[step], in_up.at[step, :, inner, :], (0, 1)),
-            (out_down.at[step], in_down.at[step, :, inner, :], (0, -1)),
-        ]
-        for c, (i, plane, dx, dy) in enumerate(CORNERS):
-            moves.append((post.at[PLACE[i], plane], in_corner.at[step, c], (dx, dy)))
+        moves = []
+        for i, plane, dx, dy in CORNERS:
+            row = NY - 1 if dy == 1 else 0
+            src = post.at[PLACE[i], plane, pl.ds(row, 1), :]
+            at = pl.ds(HALO0 - 1 if dx == 1 else HALO0 + NX, 1)
+            if dy == 1:
+                dst = in_up.at[step, Y_UP.index(i), at, :]
+            else:
+                dst = in_down.at[step, Y_DOWN.index(i), at, :]
+            moves.append((src, dst, (dx, dy)))
+        moves.append((post.at[pl.ds(0, 5), NX], post.at[pl.ds(0, 5), 0], (1, 0)))
+        moves.append((post.at[pl.ds(5, 5), 1], post.at[pl.ds(5, 5), NX + 1], (-1, 0)))
+        for first in (0, NX // 2):
+            src, dst = pl.ds(first, NX // 2), pl.ds(HALO0 + first, NX // 2)
+            moves.append((out_up.at[step, :, src, :], in_up.at[step, :, dst, :], (0, 1)))
+            moves.append((out_down.at[step, :, src, :], in_down.at[step, :, dst, :], (0, -1)))
         return [
             pltpu.make_async_remote_copy(
                 src_ref=src,
@@ -307,22 +310,15 @@
             for k, (src, dst, to) in enumerate(moves)
         ]
 
-    def land(step):
-        for c, (i, plane, dx, dy) in enumerate(CORNERS):
-            at = HALO0 - 1 if dx == 1 else HALO0 + NX
-            if dy == 1:
-                in_up[step, Y_UP.index(i), at : at + 1, :] = in_corner[step, c, NY - 1 : NY, :]
-            else:
-                in_down[step, Y_DOWN.index(i), at : at + 1, :] = in_corner[step, c, 0:1, :]
-
     loads[0].wait()
     loads[1].wait()
-
-    @pl.loop(0, NX)
-    def _(x):
-        load_plane(x).wait()
-        field = [pops[i, x] for i in range(19)]
-        put(collide(field, rate[x], mask[x] > 0), 0, x)
+    for g in range(NX // 4):
+        load_planes(g).wait()
+
+        @pl.loop(4 * g, 4 * g + 4)
+        def _(x):
+            field = [pops[i, x] for i in range(19)]
+            put(collide(field, rate[x], mask[x] > 0), 0, x)
 
     pl.semaphore_wait(barrier, (nx - 1) + (ny - 1) + 4)
     first = halo(0)
@@ -373,15 +369,25 @@
 
     for copy in first:
         copy.wait_recv()
-    land(0)
+    second = halo(1)
 
     @pl.loop(0, NX)
-    def _(x):
+    def _(k):
+        x = lax.rem(k + (NX - 1), NX)
         field = arrive(post_a, in_up.at[0], in_down.at[0], x)
         put(collide(field, rate[x], mask[x] > 0), 1, x)
 
-    second = halo(1)
-    for copy in second:
+        @pl.when(k == 1)
+        def _():
+            for copy in second[0:6]:
+                copy.start()
+
+        @pl.when(k == NX // 2)
+        def _():
+            for copy in second[6:8]:
+                copy.start()
+
+    for copy in second[8:10]:
         copy.start()
 
     def all_along(src, dst, k, axis):
@@ -437,7 +443,6 @@
         recv_c[mx] = value
         start_all(ring_c, nx)
 
-    land(1)
 
     @pl.loop(0, XC)
     def _(xc):
@@ -652,7 +657,6 @@
             vmem(2, 5, NX, NZ),
             vmem(2, 5, NX + 16, NZ),
             vmem(2, 5, NX + 16, NZ),
-            vmem(2, 4, NY, NZ),
             vmem(3 * XC * NY, NZ),
             vmem(3 * XC * NY, ZC),
             vmem(2 * COLS, ZC),
@@ -669,10 +673,10 @@
             vmem(8, ZC),
             vmem(COLS, ZC),
             pltpu.VMEM((COLS, 2 * ZC), BF16),
-            dma((NX,)),
+            dma((NX // 4,)),
             dma((5,)),
-            dma((2, 8)),
-            dma((2, 8)),
+            dma((2, 10)),
+            dma((2, 10)),
             dma((5,)),
             dma((5,)),
         ],

time: 41.5 us -> 40.3 us (0.971)
  Pallas kernels: 40.7 us -> 39.6 us
    pallas_call x1, Pallas kernels: 37.4 us -> 36.2 us  [on_device(): pl.pallas_call(functools.partial(main_kernel, nx, ny), out_shape=(f32(19,...]
where the time goes in v2:
time: 40.3 us; the launch traced here: 40.2 us
  Pallas kernels  39.6 us (98%)
  between operations  0.64 us (2%)
    pallas_call x1, Pallas kernels, on_device(): pl.pallas_call(functools.partial(main_kernel, nx, ny), out_shape=(f32(19,...  36.2 us
    pallas_call x1, Pallas kernels, on_device(): pl.pallas_call(finish_kernel, out_shape=(f32(19, NX, NY, NZ), f32(COLS, C...  3.38 us

profile of v2, /device:TPU:1, one launch (start us, length us, event | category | flops | bytes accessed | tf_op | source)
XLA Modules:
  0.0 40.2 jit_solution(15655665375167822224)
XLA Ops:
  0.6 36.2 %substeps.1 = (f32[19,16,8,256]{3,2,1,0:T(8,128)S(1)}, f32[80,104,128]{2,1,0:T(8,128)S(1)}, f32[96,128]{1,0:T(8,128)S(1)}, f32[80,128]{1,0:T(8,128)S(1)}, f32[80,128]{1,0:T(8,128)S(1)}, /*index=5*/f32[8,128]{1,0:T(8,128)S(1)}) custom-call(f32[19,16,8,256]{3,2,1,0:T(8,128)} %pops_hbm.1, f32[16,8,256]{2,1,0:T(8,128)} %rate_hbm.1, s32[16,8,256]{2,1,0:T(8,128)} %mask_hbm.1, ...), custom_call_target="tpu_custom_call" | custom-call | tf_op jit(solution)/shard_map/substeps/pallas_call | solution.py:637
  36.8 3.4 %finish.1 = (f32[19,16,8,256]{3,2,1,0:T(8,128)}, f32[80,80]{1,0:T(8,128)}, f32[80,96,128]{2,1,0:T(8,128)}) custom-call(f32[19,16,8,256]{3,2,1,0:T(8,128)S(1)} %get-tuple-element.12.field_ref, f32[80,104,128]{2,1,0:T(8,128)S(1)} %get-tuple-element.13.fresh_ref, f32[96,128]{1,0:T(8,128)S(1)} %get-tuple-element.14.coarse_ref, ...), custom_call_target="tpu_custom_call" | custom-call | tf_op jit(solution)/shard_map/finish/pallas_call | solution.py:688

commit v3 on v2

--- a/solution.py
+++ b/solution.py
@@ -114,10 +114,33 @@
     return field
 
 
+def arrive_face(post_ref, up_ref, down_ref, y):
+    field = []
+    for i, (cx, cy, cz) in enumerate(VELOCITY):
+        if 0 <= y - cy < NY:
+            v = post_ref[PLACE[i], 1 - cx : 1 - cx + NX, y - cy, :]
+        elif cy == 1:
+            v = up_ref[Y_UP.index(i), HALO0 - cx : HALO0 - cx + NX, :]
+        else:
+            v = down_ref[Y_DOWN.index(i), HALO0 - cx : HALO0 - cx + NX, :]
+        if cz == 1:
+            v = pltpu.roll(v, 1, axis=1)
+        elif cz == -1:
+            v = pltpu.roll(v, NZ - 1, axis=1)
+        field.append(v)
+    return field
+
+
 def split(x):
     hi = x.astype(BF16)
     lo = (x - hi.astype(F32)).astype(BF16)
     return hi, lo
+
+
+def tall(rows, c, wide):
+    return jnp.concatenate(
+        [rows[pl.ds(c * wide + w, COLS, stride=PITCH), :] for w in range(wide)], axis=1
+    )
 
 
 def dot(a, b, ca, cb, precision=None):
@@ -187,15 +210,13 @@
     basis_hbm,
     snaps_hbm,
     field_out,
-    fresh,
-    coarse_ref,
+    stack,
     inverse_ref,
     upper_ref,
     border_ref,
     pops,
     rate,
     mask,
-    stack,
     post_a,
     post_b,
     out_up,
@@ -217,7 +238,6 @@
     sv,
     scale,
     work,
-    left,
     plane_sem,
     load_sem,
     halo_send,
@@ -275,6 +295,8 @@
     def put(post, step, x):
         for i in range(19):
             posts[step][PLACE[i], x + 1] = post[i]
+
+    def put_rows(post, step, x):
         for p, i in enumerate(Y_UP):
             out_up[step, p, pl.ds(x, 1), :] = post[i][NY - 1 : NY, :]
         for p, i in enumerate(Y_DOWN):
@@ -284,20 +306,21 @@
         post = posts[step]
         moves = []
         for i, plane, dx, dy in CORNERS:
-            row = NY - 1 if dy == 1 else 0
-            src = post.at[PLACE[i], plane, pl.ds(row, 1), :]
+            from_row = pl.ds(plane - 1, 1)
             at = pl.ds(HALO0 - 1 if dx == 1 else HALO0 + NX, 1)
             if dy == 1:
-                dst = in_up.at[step, Y_UP.index(i), at, :]
+                p = Y_UP.index(i)
+                moves.append((out_up.at[step, p, from_row, :], in_up.at[step, p, at, :], (dx, dy)))
             else:
-                dst = in_down.at[step, Y_DOWN.index(i), at, :]
-            moves.append((src, dst, (dx, dy)))
+                p = Y_DOWN.index(i)
+                moves.append(
+                    (out_down.at[step, p, from_row, :], in_down.at[step, p, at, :], (dx, dy))
+                )
+        inner = pl.ds(HALO0, NX)
+        moves.append((out_up.at[step], in_up.at[step, :, inner, :], (0, 1)))
+        moves.append((out_down.at[step], in_down.at[step, :, inner, :], (0, -1)))
         moves.append((post.at[pl.ds(0, 5), NX], post.at[pl.ds(0, 5), 0], (1, 0)))
         moves.append((post.at[pl.ds(5, 5), 1], post.at[pl.ds(5, 5), NX + 1], (-1, 0)))
-        for first in (0, NX // 2):
-            src, dst = pl.ds(first, NX // 2), pl.ds(HALO0 + first, NX // 2)
-            moves.append((out_up.at[step, :, src, :], in_up.at[step, :, dst, :], (0, 1)))
-            moves.append((out_down.at[step, :, src, :], in_down.at[step, :, dst, :], (0, -1)))
         return [
             pltpu.make_async_remote_copy(
                 src_ref=src,
@@ -318,7 +341,9 @@
         @pl.loop(4 * g, 4 * g + 4)
         def _(x):
             field = [pops[i, x] for i in range(19)]
-            put(collide(field, rate[x], mask[x] > 0), 0, x)
+            post = collide(field, rate[x], mask[x] > 0)
+            put(post, 0, x)
+            put_rows(post, 0, x)
 
     pl.semaphore_wait(barrier, (nx - 1) + (ny - 1) + 4)
     first = halo(0)
@@ -331,14 +356,9 @@
     rows = stack.reshape(COLS * PITCH, ZC)
     gram[...] = jnp.zeros_like(gram)
 
-    def tall(c, wide):
-        return jnp.concatenate(
-            [rows[pl.ds(c * wide + w, COLS, stride=PITCH), :] for w in range(wide)], axis=1
-        )
-
     @pl.loop(0, ROWS // 32)
     def _(c):
-        hi, lo = split(tall(c, 32))
+        hi, lo = split(tall(rows, c, 32))
         gram[:, 0:COLS] += dot(jnp.concatenate([hi, lo], axis=0), hi, 1, 1)
 
     low = jnp.concatenate([gram[COLS : 2 * COLS, :], jnp.zeros((ZC - COLS, ZC), F32)], axis=0)
@@ -370,6 +390,13 @@
     for copy in first:
         copy.wait_recv()
     second = halo(1)
+    for y, group, out in ((NY - 1, Y_UP, out_up), (0, Y_DOWN, out_down)):
+        field = arrive_face(post_a, in_up.at[0], in_down.at[0], y)
+        post = collide(field, rate[:, y, :], mask[:, y, :] > 0)
+        for p, i in enumerate(group):
+            out[1, p] = post[i]
+    for copy in second[0:6]:
+        copy.start()
 
     @pl.loop(0, NX)
     def _(k):
@@ -379,16 +406,8 @@
 
         @pl.when(k == 1)
         def _():
-            for copy in second[0:6]:
-                copy.start()
-
-        @pl.when(k == NX // 2)
-        def _():
             for copy in second[6:8]:
                 copy.start()
-
-    for copy in second[8:10]:
-        copy.start()
 
     def all_along(src, dst, k, axis):
         def copy(j):
@@ -435,14 +454,6 @@
     for copy in second:
         copy.wait_recv()
 
-    @pl.when(mx < owners)
-    def _():
-        wait_for(recv_b.at[pl.ds(0, ny - 1)], red_recv.at[1])
-        value = total(recv_b, ny)
-        send_b[1] = value
-        recv_c[mx] = value
-        start_all(ring_c, nx)
-
 
     @pl.loop(0, XC)
     def _(xc):
@@ -459,12 +470,19 @@
         for a in range(3):
             vel[pl.ds(pl.multiple_of(a * XC * NY + xc * NY, NY), NY), :] = sums[a]
 
+    @pl.when(mx < owners)
+    def _():
+        wait_for(recv_b.at[pl.ds(0, ny - 1)], red_recv.at[1])
+        value = total(recv_b, ny)
+        send_b[1] = value
+        recv_c[mx] = value
+        start_all(ring_c, nx)
+
     fine = lax.broadcasted_iota(jnp.int32, (NZ, ZC), 0)
     pair = lax.broadcasted_iota(jnp.int32, (NZ, ZC), 1)
     pick = jnp.where(fine // 2 == pair, SPEED_SCALE / 8.0, 0.0).astype(F32)
     pooled[...] = dot(vel[...], pick, 1, 0, HIGHEST)
     coarse = pooled[pl.ds(0, ROWS, stride=2), :] + pooled[pl.ds(1, ROWS, stride=2), :]
-    coarse_ref[...] = coarse
     stack[COLS - 1, 0:ROWS, :] = coarse
 
     tiles = ROWS // 8
@@ -487,6 +505,19 @@
     ring_d = all_along(vec_b.at[0, one], vec_in_a.at[mx, one], 3, 0)
     start_all(ring_d, nx)
 
+    def vec_total(ref, count):
+        value = ref[0, 0:1, :]
+        for j in range(1, count):
+            value = value + ref[j, 0:1, :]
+        return value
+
+    wait_for(vec_in_a.at[pl.ds(0, nx - 1), one], red_recv.at[3])
+    value = jnp.broadcast_to(vec_total(vec_in_a, nx), (8, ZC))
+    vec_b[1] = value
+    vec_in_b[my] = value
+    ring_e = all_along(vec_b.at[1, one], vec_in_b.at[my, one], 4, 1)
+    start_all(ring_e, ny)
+
     @pl.when(mx < owners)
     def _():
         wait_for(recv_c.at[pl.ds(0, owners - 1)], red_recv.at[2])
@@ -508,44 +539,16 @@
     work[...] = whole
     inverse_ref[...] = (row == lane).astype(F32)
 
-    def vec_total(ref, count):
-        value = ref[0, 0:1, :]
-        for j in range(1, count):
-            value = value + ref[j, 0:1, :]
-        return value
-
-    half = owners // 2 - 1
+    half = 0
     for b in range(half):
         factor_block(b, work, inverse_ref, upper_ref)
 
-    wait_for(vec_in_a.at[pl.ds(0, nx - 1), one], red_recv.at[3])
-    value = jnp.broadcast_to(vec_total(vec_in_a, nx), (8, ZC))
-    vec_b[1] = value
-    vec_in_b[my] = value
-    ring_e = all_along(vec_b.at[1, one], vec_in_b.at[my, one], 4, 1)
-    start_all(ring_e, ny)
-
     for b in range(half, owners):
         factor_block(b, work, inverse_ref, upper_ref)
 
-    scaled = inverse_ref[...] * srow
-    hi = scaled.astype(BF16).astype(F32)
-    lo = scaled - hi
-    none = jnp.zeros_like(hi)
-    hi, lo = jnp.concatenate([hi, none], axis=1), jnp.concatenate([lo, none], axis=1)
-    placed = hi + pltpu.roll(lo, COLS, axis=1) + pltpu.roll(hi, 2 * COLS, axis=1)
-    left[...] = placed.astype(BF16)
-    made = fresh.reshape(COLS * PITCH, ZC)
-
-    @pl.loop(0, ROWS // 16)
-    def _(c):
-        hi, lo = split(tall(c, 16))
-        result = dot(left[:, 0 : 3 * COLS], jnp.concatenate([hi, hi, lo], axis=0), 1, 0)
-        for w in range(16):
-            made[pl.ds(c * 16 + w, COLS, stride=PITCH), :] = result[:, w * ZC : (w + 1) * ZC]
-
     wait_for(vec_in_b.at[pl.ds(0, ny - 1), one], red_recv.at[4])
-    border_ref[...] = jnp.broadcast_to(vec_total(vec_in_b, ny) * srow * per_row, (8, ZC))
+    border_ref[0:4, :] = jnp.broadcast_to(vec_total(vec_in_b, ny) * srow * per_row, (4, ZC))
+    border_ref[4:8, :] = jnp.broadcast_to(srow, (4, ZC))
 
     for copy in first + second:
         copy.wait_send()
@@ -570,51 +573,64 @@
 
 def finish_kernel(
     field_ref,
-    fresh_ref,
-    coarse_ref,
+    stack,
     inverse_ref,
     upper_ref,
     border_ref,
     pops_hbm,
     factor_ref,
     new_hbm,
-    column,
-    newest,
+    fresh,
+    left,
     sem,
 ):
-    done = pl.ds(0, COLS - 1)
-    copies = [
-        pltpu.make_async_copy(fresh_ref.at[done, pl.ds(0, ROWS)], new_hbm.at[done], sem.at[0]),
-        pltpu.make_async_copy(field_ref, pops_hbm, sem.at[1]),
-        pltpu.make_async_copy(newest, new_hbm.at[COLS - 1], sem.at[2]),
-    ]
-    copies[0].start()
-    copies[1].start()
+    wide = 16
+    field = pltpu.make_async_copy(field_ref, pops_hbm, sem.at[ROWS // wide])
+    field.start()
 
     row = lax.broadcasted_iota(jnp.int32, (COLS, ZC), 0)
     lane = lax.broadcasted_iota(jnp.int32, (COLS, ZC), 1)
     inverse = inverse_ref[...]
-    border = border_ref[...]
-    lane8 = lax.broadcasted_iota(jnp.int32, (8, ZC), 1)
-    old = jnp.where(lane8 < COLS - 1, border, 0.0)
-    lcol = dot(inverse, jnp.concatenate([old] * (ZC // 8), axis=0), 1, 1, HIGHEST)
+    border = border_ref[0:1, :]
+    scale = border_ref[4:5, :]
+    old = jnp.where(lane[0:1] < COLS - 1, border, 0.0)
+    lcol = dot(inverse, jnp.broadcast_to(old, (ZC, ZC)), 1, 1, HIGHEST)
     lcol = jnp.where(row < COLS - 1, lcol, 0.0)
-    column[...] = lcol
     square = border[0:1, COLS - 1 : COLS] - jnp.sum(lcol * lcol, axis=0, keepdims=True)
     inv = lax.rsqrt(square)
     end = jnp.where(row == COLS - 1, square * inv, lcol)
     factor_ref[...] = jnp.where(lane == COLS - 1, end, upper_ref[...])[:, 0:COLS]
-
-    def minus(k, value):
-        for q in range(8):
-            i = k * 8 + q
-            value = value - column[pl.ds(i, 1), :] * fresh_ref[i, 0:ROWS, :]
-        return value
-
-    newest[...] = lax.fori_loop(0, COLS // 8, minus, coarse_ref[...]) * inv
-    copies[2].start()
-    for copy in copies:
-        copy.wait()
+    bottom = jnp.sum(lcol * inverse, axis=0, keepdims=True)
+    bottom = jnp.where(lane[0:1] == COLS - 1, inv, -bottom * inv)
+    inverse = jnp.where(row == COLS - 1, bottom, inverse) * scale
+
+    hi = inverse.astype(BF16).astype(F32)
+    lo = inverse - hi
+    none = jnp.zeros_like(hi)
+    hi, lo = jnp.concatenate([hi, none], axis=1), jnp.concatenate([lo, none], axis=1)
+    placed = hi + pltpu.roll(lo, COLS, axis=1) + pltpu.roll(hi, 2 * COLS, axis=1)
+    left[...] = placed.astype(BF16)
+
+    rows = stack.reshape(COLS * PITCH, ZC)
+    made = fresh.reshape(COLS * PITCH, ZC)
+
+    def store(c):
+        part = pl.ds(pl.multiple_of(c * wide, wide), wide)
+        return pltpu.make_async_copy(fresh.at[:, part], new_hbm.at[:, part], sem.at[c])
+
+    @pl.loop(0, ROWS // wide)
+    def _(c):
+        hi, lo = split(tall(rows, c, wide))
+        result = dot(left[:, 0 : 3 * COLS], jnp.concatenate([hi, hi, lo], axis=0), 1, 0)
+        for w in range(wide):
+            made[pl.ds(c * wide + w, COLS, stride=PITCH), :] = result[:, w * ZC : (w + 1) * ZC]
+        store(c).start()
+
+    @pl.loop(0, ROWS // wide)
+    def _(c):
+        store(c).wait()
+
+    field.wait()
 
 
 def on_device(nx, ny, pops, rate, mask, sv, basis, snaps):
@@ -634,23 +650,21 @@
         return pltpu.VMEM(shape, F32)
 
     dma = pltpu.SemaphoreType.DMA
-    field, fresh, coarse, inverse, upper, border = pl.pallas_call(
+    field, stack, inverse, upper, border = pl.pallas_call(
         functools.partial(main_kernel, nx, ny),
         out_shape=(
             f32(19, NX, NY, NZ),
             f32(COLS, PITCH, ZC),
-            f32(ROWS, ZC),
             f32(COLS, ZC),
             f32(COLS, ZC),
             f32(8, ZC),
         ),
         in_specs=[far] * 6,
-        out_specs=(here,) * 6,
+        out_specs=(here,) * 5,
         scratch_shapes=[
             vmem(19, NX, NY, NZ),
             vmem(NX, NY, NZ),
             pltpu.VMEM((NX, NY, NZ), jnp.int32),
-            vmem(COLS, PITCH, ZC),
             vmem(19, NX + 2, NY, NZ),
             vmem(19, NX + 2, NY, NZ),
             vmem(2, 5, NX, NZ),
@@ -672,11 +686,10 @@
             vmem(1, RANK),
             vmem(8, ZC),
             vmem(COLS, ZC),
-            pltpu.VMEM((COLS, 2 * ZC), BF16),
             dma((NX // 4,)),
             dma((5,)),
-            dma((2, 10)),
-            dma((2, 10)),
+            dma((2, 8)),
+            dma((2, 8)),
             dma((5,)),
             dma((5,)),
         ],
@@ -688,12 +701,16 @@
     out, factor, new = pl.pallas_call(
         finish_kernel,
         out_shape=(f32(19, NX, NY, NZ), f32(COLS, COLS), f32(COLS, ROWS, ZC)),
-        in_specs=[here] * 6,
+        in_specs=[here] * 5,
         out_specs=(far, here, far),
-        scratch_shapes=[vmem(COLS, ZC), vmem(ROWS, ZC), dma((3,))],
-        compiler_params=pltpu.CompilerParams(vmem_limit_bytes=16 * 2**20),
+        scratch_shapes=[
+            vmem(COLS, PITCH, ZC),
+            pltpu.VMEM((COLS, 2 * ZC), BF16),
+            dma((ROWS // 16 + 1,)),
+        ],
+        compiler_params=pltpu.CompilerParams(vmem_limit_bytes=24 * 2**20),
         name="finish",
-    )(field, fresh, coarse, inverse, upper, border)
+    )(field, stack, inverse, upper, border)
     return out, factor, new.reshape(COLS, 3, XC, YC, ZC)
 
 

time: 40.3 us -> 38.4 us (0.953)
  Pallas kernels: 39.6 us -> 37.6 us
    pallas_call x1, Pallas kernels: 36.2 us -> 33.8 us  [on_device(): pl.pallas_call(functools.partial(main_kernel, nx, ny), out_shape=(f32(19,...]
    pallas_call x1, Pallas kernels: 3.38 us -> 3.81 us  [on_device(): pl.pallas_call(finish_kernel, out_shape=(f32(19, NX, NY, NZ), f32(COLS, C...]
where the time goes in v3:
time: 38.4 us; the launch traced here: 38.3 us
  Pallas kernels  37.6 us (98%)
  between operations  0.64 us (2%)
    pallas_call x1, Pallas kernels, on_device(): pl.pallas_call(functools.partial(main_kernel, nx, ny), out_shape=(f32(19,...  33.8 us
    pallas_call x1, Pallas kernels, on_device(): pl.pallas_call(finish_kernel, out_shape=(f32(19, NX, NY, NZ), f32(COLS, C...  3.81 us

profile of v3, /device:TPU:1, one launch (start us, length us, event | category | flops | bytes accessed | tf_op | source)
XLA Modules:
  0.0 38.3 jit_solution(3909884002617237925)
XLA Ops:
  0.6 33.8 %substeps.1 = (f32[19,16,8,256]{3,2,1,0:T(8,128)S(1)}, f32[80,104,128]{2,1,0:T(8,128)S(1)}, f32[80,128]{1,0:T(8,128)S(1)}, f32[80,128]{1,0:T(8,128)S(1)}, f32[8,128]{1,0:T(8,128)S(1)}) custom-call(f32[19,16,8,256]{3,2,1,0:T(8,128)} %pops_hbm.1, f32[16,8,256]{2,1,0:T(8,128)} %rate_hbm.1, s32[16,8,256]{2,1,0:T(8,128)} %mask_hbm.1, f32[1,64]{1,0:T(1,128)} %bitcast.6, ...), custom_call_target="tpu_custom_call" | custom-call | tf_op jit(solution)/shard_map/substeps/pallas_call | solution.py:653
  34.5 3.8 %finish.1 = (f32[19,16,8,256]{3,2,1,0:T(8,128)}, f32[80,80]{1,0:T(8,128)}, f32[80,96,128]{2,1,0:T(8,128)}) custom-call(f32[19,16,8,256]{3,2,1,0:T(8,128)S(1)} %get-tuple-element.11.field_ref, f32[80,104,128]{2,1,0:T(8,128)S(1)} %get-tuple-element.12.stack, f32[80,128]{1,0:T(8,128)S(1)} %get-tuple-element.13.inverse_ref, ...), custom_call_target="tpu_custom_call" | custom-call | tf_op jit(solution)/shard_map/finish/pallas_call | solution.py:701

commit v4 on v3

--- a/solution.py
+++ b/solution.py
@@ -214,6 +214,7 @@
     inverse_ref,
     upper_ref,
     border_ref,
+    left,
     pops,
     rate,
     mask,
@@ -546,9 +547,16 @@
     for b in range(half, owners):
         factor_block(b, work, inverse_ref, upper_ref)
 
+    inverse = inverse_ref[...] * srow
+    hi = inverse.astype(BF16).astype(F32)
+    lo = inverse - hi
+    none = jnp.zeros_like(hi)
+    hi, lo = jnp.concatenate([hi, none], axis=1), jnp.concatenate([lo, none], axis=1)
+    placed = hi + pltpu.roll(lo, COLS, axis=1) + pltpu.roll(hi, 2 * COLS, axis=1)
+    left[...] = placed.astype(BF16)
+
     wait_for(vec_in_b.at[pl.ds(0, ny - 1), one], red_recv.at[4])
-    border_ref[0:4, :] = jnp.broadcast_to(vec_total(vec_in_b, ny) * srow * per_row, (4, ZC))
-    border_ref[4:8, :] = jnp.broadcast_to(srow, (4, ZC))
+    border_ref[...] = jnp.broadcast_to(vec_total(vec_in_b, ny) * srow * per_row, (8, ZC))
 
     for copy in first + second:
         copy.wait_send()
@@ -577,46 +585,27 @@
     inverse_ref,
     upper_ref,
     border_ref,
+    left,
     pops_hbm,
     factor_ref,
     new_hbm,
     fresh,
-    left,
+    column,
+    newest,
     sem,
 ):
-    wide = 16
+    wide = 32
     field = pltpu.make_async_copy(field_ref, pops_hbm, sem.at[ROWS // wide])
     field.start()
 
-    row = lax.broadcasted_iota(jnp.int32, (COLS, ZC), 0)
-    lane = lax.broadcasted_iota(jnp.int32, (COLS, ZC), 1)
-    inverse = inverse_ref[...]
-    border = border_ref[0:1, :]
-    scale = border_ref[4:5, :]
-    old = jnp.where(lane[0:1] < COLS - 1, border, 0.0)
-    lcol = dot(inverse, jnp.broadcast_to(old, (ZC, ZC)), 1, 1, HIGHEST)
-    lcol = jnp.where(row < COLS - 1, lcol, 0.0)
-    square = border[0:1, COLS - 1 : COLS] - jnp.sum(lcol * lcol, axis=0, keepdims=True)
-    inv = lax.rsqrt(square)
-    end = jnp.where(row == COLS - 1, square * inv, lcol)
-    factor_ref[...] = jnp.where(lane == COLS - 1, end, upper_ref[...])[:, 0:COLS]
-    bottom = jnp.sum(lcol * inverse, axis=0, keepdims=True)
-    bottom = jnp.where(lane[0:1] == COLS - 1, inv, -bottom * inv)
-    inverse = jnp.where(row == COLS - 1, bottom, inverse) * scale
-
-    hi = inverse.astype(BF16).astype(F32)
-    lo = inverse - hi
-    none = jnp.zeros_like(hi)
-    hi, lo = jnp.concatenate([hi, none], axis=1), jnp.concatenate([lo, none], axis=1)
-    placed = hi + pltpu.roll(lo, COLS, axis=1) + pltpu.roll(hi, 2 * COLS, axis=1)
-    left[...] = placed.astype(BF16)
-
     rows = stack.reshape(COLS * PITCH, ZC)
     made = fresh.reshape(COLS * PITCH, ZC)
 
+    done = pl.ds(0, COLS - 1)
+
     def store(c):
         part = pl.ds(pl.multiple_of(c * wide, wide), wide)
-        return pltpu.make_async_copy(fresh.at[:, part], new_hbm.at[:, part], sem.at[c])
+        return pltpu.make_async_copy(fresh.at[done, part], new_hbm.at[done, part], sem.at[c])
 
     @pl.loop(0, ROWS // wide)
     def _(c):
@@ -625,6 +614,31 @@
         for w in range(wide):
             made[pl.ds(c * wide + w, COLS, stride=PITCH), :] = result[:, w * ZC : (w + 1) * ZC]
         store(c).start()
+
+    row = lax.broadcasted_iota(jnp.int32, (COLS, ZC), 0)
+    lane = lax.broadcasted_iota(jnp.int32, (COLS, ZC), 1)
+    inverse = inverse_ref[...]
+    border = border_ref[0:1, :]
+    old = jnp.where(lane[0:1] < COLS - 1, border, 0.0)
+    lcol = dot(inverse, jnp.broadcast_to(old, (ZC, ZC)), 1, 1, HIGHEST)
+    lcol = jnp.where(row < COLS - 1, lcol, 0.0)
+    column[...] = lcol
+    square = border[0:1, COLS - 1 : COLS] - jnp.sum(lcol * lcol, axis=0, keepdims=True)
+    inv = lax.rsqrt(square)
+    end = jnp.where(row == COLS - 1, square * inv, lcol)
+    factor_ref[...] = jnp.where(lane == COLS - 1, end, upper_ref[...])[:, 0:COLS]
+
+    def minus(k, value):
+        for q in range(8):
+            i = k * 8 + q
+            value = value - column[pl.ds(i, 1), :] * fresh[i, 0:ROWS, :]
+        return value
+
+    value = stack[COLS - 1, 0:ROWS, :]
+    newest[...] = lax.fori_loop(0, COLS // 8, minus, value) * inv
+    last = pltpu.make_async_copy(newest, new_hbm.at[COLS - 1], sem.at[ROWS // wide + 1])
+    last.start()
+    last.wait()
 
     @pl.loop(0, ROWS // wide)
     def _(c):
@@ -650,7 +664,7 @@
         return pltpu.VMEM(shape, F32)
 
     dma = pltpu.SemaphoreType.DMA
-    field, stack, inverse, upper, border = pl.pallas_call(
+    field, stack, inverse, upper, border, left = pl.pallas_call(
         functools.partial(main_kernel, nx, ny),
         out_shape=(
             f32(19, NX, NY, NZ),
@@ -658,9 +672,10 @@
             f32(COLS, ZC),
             f32(COLS, ZC),
             f32(8, ZC),
+            jax.ShapeDtypeStruct((COLS, 2 * ZC), BF16),
         ),
         in_specs=[far] * 6,
-        out_specs=(here,) * 5,
+        out_specs=(here,) * 6,
         scratch_shapes=[
             vmem(19, NX, NY, NZ),
             vmem(NX, NY, NZ),
@@ -701,16 +716,17 @@
     out, factor, new = pl.pallas_call(
         finish_kernel,
         out_shape=(f32(19, NX, NY, NZ), f32(COLS, COLS), f32(COLS, ROWS, ZC)),
-        in_specs=[here] * 5,
+        in_specs=[here] * 6,
         out_specs=(far, here, far),
         scratch_shapes=[
             vmem(COLS, PITCH, ZC),
-            pltpu.VMEM((COLS, 2 * ZC), BF16),
-            dma((ROWS // 16 + 1,)),
+            vmem(COLS, ZC),
+            vmem(ROWS, ZC),
+            dma((ROWS // 16 + 2,)),
         ],
         compiler_params=pltpu.CompilerParams(vmem_limit_bytes=24 * 2**20),
         name="finish",
-    )(field, stack, inverse, upper, border)
+    )(field, stack, inverse, upper, border, left)
     return out, factor, new.reshape(COLS, 3, XC, YC, ZC)
 
 

time: 38.4 us -> 38.1 us (level)
  no operation moved by 1% of the time
where the time goes in v4:
time: 38.1 us
  Pallas kernels  37.4 us (98%)
  between operations  0.64 us (2%)
    pallas_call x1, Pallas kernels, on_device(): pl.pallas_call(functools.partial(main_kernel, nx, ny), out_shape=(f32(19,...  33.9 us
    pallas_call x1, Pallas kernels, on_device(): pl.pallas_call(finish_kernel, out_shape=(f32(19, NX, NY, NZ), f32(COLS, C...  3.54 us

profile of v4, /device:TPU:1, one launch (start us, length us, event | category | flops | bytes accessed | tf_op | source)
XLA Modules:
  0.0 38.1 jit_solution(846987969579621693)
XLA Ops:
  0.6 33.9 %substeps.1 = (f32[19,16,8,256]{3,2,1,0:T(8,128)S(1)}, f32[80,104,128]{2,1,0:T(8,128)S(1)}, f32[80,128]{1,0:T(8,128)S(1)}, f32[80,128]{1,0:T(8,128)S(1)}, f32[8,...) custom-call(f32[19,16,8,256]{3,2,1,0:T(8,128)} %pops_hbm.1, f32[16,8,256]{2,1,0:T(8,128)} %rate_hbm.1, ...), custom_call_target="tpu_custom_call" | custom-call | tf_op jit(solution)/shard_map/substeps/pallas_call | solution.py:667
  34.5 3.5 %finish.1 = (f32[19,16,8,256]{3,2,1,0:T(8,128)}, f32[80,80]{1,0:T(8,128)}, f32[80,96,128]{2,1,0:T(8,128)}) custom-call(f32[19,16,8,256]{3,2,1,0:T(8,128)S(1)} %get-tuple-element.12.field_ref, f32[80,104,128]{2,1,0:T(8,128)S(1)} %get-tuple-element.13.stack, f32[80,128]{1,0:T(8,128)S(1)} %get-tuple-element.14.inverse_ref, ...), custom_call_target="tpu_custom_call" | custom-call | tf_op jit(solution)/shard_map/finish/pallas_call | solution.py:716
